TPU v7x, 256 devices: a whole 4x4x8 slice. The times are simulated.
256 devices in a mesh: coil: 16 (over y, x_lo, core), slab: 16 (over z, x_hi).
Axes of the slice: x: 4 (x_hi: 2, x_lo: 2; x = x_hi * 2 + x_lo), y: 4, z: 8, core: 2. Of those that a mesh axis runs over, the one named last changes fastest.
Arguments:
- estimate: float32 [2, 128, 128, 128], P(None, 'slab', 'coil'), may hold values from -6 to 6
- coil_maps: float32 [32, 2, 128, 128, 128], P('coil', None, 'slab'), may hold values from -2 to 2
- measured: float32 [32, 2, 128, 128, 128], P('coil', None, None, 'slab'), may hold values from -3 to 3
- line_mask: int32 [128, 128], replicated, may hold values 0 or 1
- w_first: float32 [27, 32, 2], replicated, may hold values from -0.875 to 0.875
- w_middle: float32 [27, 32, 32], replicated, may hold values from -0.21875 to 0.21875
- w_last: float32 [27, 2, 32], replicated, may hold values from -0.21875 to 0.21875
Outputs:
- combined: float32 [2, 128, 128, 128], P(None, 'slab', 'coil')
- refined: float32 [2, 128, 128, 128], P(None, 'slab', 'coil')
Inputs may be any that keep to these rules, and one draw needn't show every extreme that they name: `line_mask`: 1 marks a sampled line.
All inputs are finite; a program needn't handle non-finite values.
Results may differ from a plain program's by a relative error of at most 0.0001.
Values sent between devices are 32-bit elements; how exact they have to be, the bound alone decides.
A program may use at most 192 MiB of HBM per device.

v0:
```python
import math

import jax
import jax.numpy as jnp
from jax import lax
from jax.sharding import PartitionSpec as P


def padded_2(value, sides, width):
    for axis, dim in sides:
        count, length = (lax.axis_size(axis), value.shape[dim])
        up = [(i, (i + 1) % count) for i in range(count - 1)]
        down = [(j, i) for i, j in up]
        last = lax.slice_in_dim(value, length - width, length, axis=dim)
        first = lax.slice_in_dim(value, 0, width, axis=dim)
        before = lax.ppermute(last, axis, up)
        after = lax.ppermute(first, axis, down)
        value = jnp.concatenate([before, value, after], axis=dim)
    return value


def dft_tables(length):
    counter = jnp.arange(length, dtype=jnp.int32)
    product = counter[:, None] * counter[None, :] % length
    angles = product.astype(jnp.float32) * (2.0 * math.pi / length)
    factor = 1.0 / math.sqrt(length)
    return (jnp.cos(angles) * factor, jnp.sin(angles) * factor)


def transform(real_part, imag_part, position, inverse):
    cos_table, sine_table = dft_tables(real_part.shape[position])
    letters = "pqrs"[: real_part.ndim]
    source = letters[:position] + "n" + letters[position + 1 :]
    target = letters[:position] + "k" + letters[position + 1 :]
    formula = "kn," + source + "->" + target

    def apply_table(table, values):
        return jnp.einsum(formula, table, values, precision=lax.Precision.HIGHEST)

    factor = -1.0 if inverse else 1.0
    new_real = apply_table(cos_table, real_part) + factor * apply_table(sine_table, imag_part)
    new_imag = apply_table(cos_table, imag_part) - factor * apply_table(sine_table, real_part)
    return (new_real, new_imag)


def depth_forward(items):
    new_real, new_imag = transform(items[:, 0], items[:, 1], 1, False)
    return jnp.stack([new_real, new_imag], 1)


def plane_inverse(items):
    new_real, new_imag = transform(items[:, 0], items[:, 1], 2, True)
    new_real, new_imag = transform(new_real, new_imag, 3, True)
    return jnp.stack([new_real, new_imag], 1)


def conv_valid(padded, weights):
    widened = jnp.pad(padded, ((0, 0), (0, 0), (0, 0), (1, 1)))
    depth = padded.shape[1] - 2
    rows_out = padded.shape[2] - 2
    columns = padded.shape[3]
    total = jnp.zeros((weights.shape[1], depth, rows_out, columns), jnp.float32)
    for offset in range(27):
        shift_z = offset // 9
        shift_x = offset // 3 % 3
        shift_y = offset % 3
        window = widened[
            :, shift_z : shift_z + depth, shift_x : shift_x + rows_out, shift_y : shift_y + columns
        ]
        total = total + jnp.einsum(
            "oc,czxy->ozxy", weights[offset], window, precision=lax.Precision.HIGHEST
        )
    return total


def layer_halo(field):
    return padded_2(field, (("coil", 2), ("slab", 1)), 1)


def body(estimate, coil_maps, measured, line_mask, w_first, w_middle, w_last):
    slab_image = lax.all_gather(estimate, "coil", axis=2, tiled=True)
    image_real = slab_image[0]
    image_imag = slab_image[1]
    map_real = coil_maps[:, 0]
    map_imag = coil_maps[:, 1]
    coil_real = map_real * image_real - map_imag * image_imag
    coil_imag = map_real * image_imag + map_imag * image_real
    coil_real, coil_imag = transform(coil_real, coil_imag, 2, False)
    coil_real, coil_imag = transform(coil_real, coil_imag, 3, False)
    stacked = jnp.stack([coil_real, coil_imag], 1)
    pencils = lax.all_to_all(stacked, "slab", split_axis=3, concat_axis=2, tiled=True)
    spectra = depth_forward(pencils)
    pencil_real = spectra[:, 0]
    pencil_imag = spectra[:, 1]
    weighting = (line_mask == 1).astype(jnp.float32)[:, None, :] * 0.5
    pencil_real = pencil_real - weighting * (pencil_real - measured[:, 0])
    pencil_imag = pencil_imag - weighting * (pencil_imag - measured[:, 1])
    pencil_real, pencil_imag = transform(pencil_real, pencil_imag, 1, True)
    corrected = jnp.stack([pencil_real, pencil_imag], 1)
    slabs = lax.all_to_all(corrected, "slab", split_axis=2, concat_axis=3, tiled=True)
    returned = plane_inverse(slabs)
    back_real = returned[:, 0]
    back_imag = returned[:, 1]
    partial_real = jnp.sum(map_real * back_real + map_imag * back_imag, axis=0)
    partial_imag = jnp.sum(map_real * back_imag - map_imag * back_real, axis=0)
    partial_value = jnp.stack([partial_real, partial_imag])
    rows_here = estimate.shape[2]
    summed = lax.psum(partial_value, "coil")
    combined = lax.dynamic_slice_in_dim(summed, lax.axis_index("coil") * rows_here, rows_here, 2)
    hidden = jax.nn.relu(conv_valid(layer_halo(combined), w_first))
    hidden = jax.nn.relu(conv_valid(layer_halo(hidden), w_middle))
    branch = conv_valid(layer_halo(hidden), w_last)
    refined = combined + branch
    return (combined, refined)


def solution(mesh):
    in_specs = (
        P(None, "slab", "coil", None),
        P("coil", None, "slab", None, None),
        P("coil", None, None, "slab", None),
        P(),
        P(),
        P(),
        P(),
    )
    out_specs = (P(None, "slab", "coil", None), P(None, "slab", "coil", None))
    return jax.shard_map(body, mesh=mesh, in_specs=in_specs, out_specs=out_specs, check_vma=False)
```

profile of v0, /device:TPU:103, one launch (start us, length us, event | category | flops | bytes accessed | tf_op | source)
XLA Modules:
  0.0 514.0 jit_solution(1705274526912826765)
XLA Ops:
  7.9 40.4 %all-gather.2.cloned.1.call-done = f32[2,8,128,128]{3,2,1,0:T(8,128)} async-done(((f32[2,8,8,128]{3,2,1,0:T(8,128)}), f32[2,8,128,128]{3,2,1,0:T(8,128)}) %all-gather.2.cloned.1.call-update) | async-done | bytes 1048592 | tf_op jit(solution)/shard_map/all_gather | solution.py:81
  48.3 1.3 slice_bitcast_fusion.7
  49.6 2.0 fusion.242
  51.6 2.0 fusion.238
  53.7 2.0 fusion.32
  55.7 1.9 fusion.240
  57.7 2.0 fusion.31
  59.7 2.2 fusion.236
  61.9 1.9 fusion.30
  63.9 1.9 fusion.29
  66.0 2.5 copy.93
  68.5 9.2 %all-to-all-start = ((f32[2,2,8,128,128]{4,2,0,1,3:T(8,128)}), f32[2,2,8,128,128]{4,2,0,1,3:T(8,128)}, u32[]{:S(2)}, u32[]{:S(2)}) async-start(f32[2,2,8,128,128]{4,2,0,1,3:T(8,128)} %copy.93), calls=%async_computation | async-start | bytes 4194304 | tf_op jit(solution)/shard_map/all_to_all | solution.py:91
  77.7 2.7 fusion.556
  80.4 2.6 copy.213
  83.1 1.4 copy.214
  84.5 42.0 %all-to-all-done = f32[2,2,8,128,128]{4,2,0,1,3:T(8,128)} async-done(((f32[2,2,8,128,128]{4,2,0,1,3:T(8,128)}), f32[2,2,8,128,128]{4,2,0,1,3:T(8,128)}, u32[]{:S(2)}, u32[]{:S(2)}) %all-to-all-start) | async-done | bytes 2097184 | tf_op jit(solution)/shard_map/all_to_all | solution.py:91
  126.4 2.8 copy.95
  129.3 1.5 fusion.557
  130.7 1.6 copy.211
  132.3 2.2 fusion.171
  134.5 2.5 copy.212
  137.1 2.6 fusion.167
  139.7 2.5 fusion.166
  145.9 1.3 fusion.26
  147.1 11.2 %fusion.24 = f32[2,1,128,8,128]{2,4,3,0,1:T(8,128)S(1)} fusion(f32[2,8,128,128]{3,2,1,0:T(8,128)S(1)} %fusion.230, f32[2,128,8,128]{1,3,2,0:T(8,128)S(1)} %fusion.166), kind=kOutput, calls=%fused_computation.71 | convolution fusion | flops 403423232 | bytes 3145728 | tf_op jit(solution)/shard_map/kn,pnrs->pkrs/dot_general | solution.py:38
  158.3 1.5 pad_maximum_fusion.1
  159.8 3.1 copy.101
  162.9 55.5 %all_to_all.36 = f32[2,2,128,8,128]{4,3,0,1,2:T(8,128)S(1)} all-to-all(f32[2,2,128,8,128]{4,3,0,1,2:T(8,128)} %copy.101), channel_id=1, replica_groups=mesh['coil'=16,'slab'=16] {'slab'}, dimensions={2} | all-to-all | bytes 4194304 | tf_op jit(solution)/shard_map/all_to_all | solution.py:100
  218.6 2.0 fusion.174
  220.6 1.9 fusion.173
  222.5 1.9 fusion.20
  224.5 2.0 fusion.22
  226.4 1.9 fusion.227
  228.4 1.9 fusion.224
  230.3 2.4 fusion.18
  232.7 2.1 fusion.160
  234.9 1.9 pad_maximum_fusion.4
  236.8 120.0 %all-reduce.5.cloned.1.call-done = f32[2,8,128,128]{3,0,2,1:T(2,128)} async-done(((f32[2,8,128,128]{3,0,2,1:T(2,128)}), f32[2,8,128,128]{3,0,2,1:T(2,128)}) %all-reduce.5.cloned.1.call-update) | async-done | bytes 1048592 | tf_op jit(solution)/shard_map/psum | solution.py:108
  357.5 1.9 collective-permute-start
  359.4 2.6 collective-permute-start.1
  362.8 2.4 collective-permute-done.1
  365.3 5.3 %collective-permute-start.2 = (f32[2,1,10,128]{3,0,2,1:T(2,128)S(1)}, f32[2,1,10,128]{3,0,2,1:T(2,128)S(1)}, u32[]{:S(2)}, u32[]{:S(2)}) collective-permute-start(f32[2,1,10,128]{3,0,2,1:T(2,128)S(1)} %get-tuple-element.28), channel_id=1, source_target_pairs={{0,1},{1,2},{2,3},{3,4},{4,5},{5,6},{6,7},{7,8},{8,9},{9,10},{10,1... | collective-permute-start | bytes 30728 | tf_op jit(solution)/shard_map/ppermute | solution.py:16
  370.6 1.9 collective-permute-start.3
  373.1 5.5 %collective-permute-done.3 = f32[2,1,10,128]{3,0,2,1:T(2,128)S(1)} collective-permute-done((f32[2,1,10,128]{3,0,2,1:T(2,128)S(1)}, f32[2,1,10,128]{3,0,2,1:T(2,128)S(1)}, u32[]{:S(2)}, u32[]{:S(2)}) %collective-permute-start.3) | collective-permute-done | bytes 10272 | tf_op jit(solution)/shard_map/ppermute | solution.py:17
  392.3 1.2 convolution_add_fusion.8
  404.5 1.3 fusion.55
  408.1 2.8 collective-permute-start.4
  410.9 3.5 collective-permute-start.5
  415.4 4.4 collective-permute-done.5
  419.9 1.9 collective-permute-start.6
  421.8 4.9 collective-permute-start.7
  428.7 3.7 collective-permute-done.7
  432.4 2.2 select_maximum_fusion.4
  446.8 1.4 convolution_bitcast_fusion.6
  455.4 1.7 fusion.58
  459.1 1.2 convolution_bitcast_fusion
  460.4 1.7 fusion.60
  462.1 1.9 collective-permute-start.8
  464.1 2.4 collective-permute-start.9
  467.2 4.1 collective-permute-done.9
  471.3 3.5 collective-permute-start.10
  474.8 3.3 collective-permute-start.11
  480.0 6.5 %collective-permute-done.11 = f32[32,1,10,128]{3,0,2,1:T(8,128)S(1)} collective-permute-done((f32[32,1,10,128]{3,0,2,1:T(8,128)S(1)}, f32[32,1,10,128]{3,0,2,1:T(8,128)S(1)}, u32[]{:S(2)}, u32[]{:S(2)}) %collective-permute-start.11) | collective-permute-done | bytes 163872 | tf_op jit(solution)/shard_map/ppermute | solution.py:17
  486.5 1.8 select_maximum_fusion
  (118 shorter events, 79.1 us)
Async XLA Ops:
  7.2 42.4 %copy-start = (f32[2,2,8,128,128]{4,3,2,1,0:T(8,128)S(1)}, f32[2,2,8,128,128]{4,3,2,1,0:T(8,128)}, u32[]{:S(2)}) copy-start(f32[2,2,8,128,128]{4,3,2,1,0:T(8,128)} %param.8) | copy-start | bytes 6291460
  7.2 41.1 %all-gather.2.cloned.1.call-start = ((), (), s32[]{:S(2)}) async-start(), calls=%async_computation.2 | async-start | bytes 1114112 | tf_op jit(solution)/shard_map/all_gather | solution.py:81
  68.5 57.9 %all-to-all-start = ((f32[2,2,8,128,128]{4,2,0,1,3:T(8,128)}), f32[2,2,8,128,128]{4,2,0,1,3:T(8,128)}, u32[]{:S(2)}, u32[]{:S(2)}) async-start(f32[2,2,8,128,128]{4,2,0,1,3:T(8,128)} %copy.93), calls=%async_computation | async-start | bytes 4194304 | tf_op jit(solution)/shard_map/all_to_all | solution.py:91
  77.7 279.1 %all-reduce.5.cloned.1.call-start = ((), (), s32[]{:S(2)}) async-start(), calls=%async_computation.3 | async-start | bytes 2097152 | tf_op jit(solution)/shard_map/psum | solution.py:108
  80.4 2.6 copy-start.5
  137.1 2.6 copy-start.1
  137.1 2.6 copy-start.2
  142.2 1.2 copy-start.3
  234.8 144.0 %copy-start.6 = (f32[27,32,2]{1,2,0:T(2,128)S(1)}, f32[27,32,2]{1,2,0:T(2,128)}, u32[]{:S(2)}) copy-start(f32[27,32,2]{1,2,0:T(2,128)} %param.11) | copy-start | bytes 20740
  357.5 5.3 %collective-permute-start = (f32[2,8,1,128]{3,0,2,1:T(2,128)S(1)}, f32[2,8,1,128]{3,0,2,1:T(2,128)S(1)}, u32[]{:S(2)}, u32[]{:S(2)}) collective-permute-start(f32[2,8,1,128]{3,0,2,1:T(2,128)S(1)} %get-tuple-element.24), channel_id=1, source_target_pairs={{0,16},{16,32},{32,48},{48,64},{64,80},{80,96},{96,112},{112,128},... | collective-permute-start | bytes 24584 | tf_op jit(solution)/shard_map/ppermute | solution.py:16
  359.4 5.9 %collective-permute-start.1 = (f32[2,8,1,128]{3,0,2,1:T(2,128)S(1)}, f32[2,8,1,128]{3,0,2,1:T(2,128)S(1)}, u32[]{:S(2)}, u32[]{:S(2)}) collective-permute-start(f32[2,8,1,128]{3,0,2,1:T(2,128)S(1)} %get-tuple-element.25), channel_id=1, source_target_pairs={{16,0},{32,16},{48,32},{64,48},{80,64},{96,80},{112,96},{128,112},... | collective-permute-start | bytes 24584 | tf_op jit(solution)/shard_map/ppermute | solution.py:17
  365.3 7.9 %collective-permute-start.2 = (f32[2,1,10,128]{3,0,2,1:T(2,128)S(1)}, f32[2,1,10,128]{3,0,2,1:T(2,128)S(1)}, u32[]{:S(2)}, u32[]{:S(2)}) collective-permute-start(f32[2,1,10,128]{3,0,2,1:T(2,128)S(1)} %get-tuple-element.28), channel_id=1, source_target_pairs={{0,1},{1,2},{2,3},{3,4},{4,5},{5,6},{6,7},{7,8},{8,9},{9,10},{10,1... | collective-permute-start | bytes 30728 | tf_op jit(solution)/shard_map/ppermute | solution.py:16
  370.6 8.0 %collective-permute-start.3 = (f32[2,1,10,128]{3,0,2,1:T(2,128)S(1)}, f32[2,1,10,128]{3,0,2,1:T(2,128)S(1)}, u32[]{:S(2)}, u32[]{:S(2)}) collective-permute-start(f32[2,1,10,128]{3,0,2,1:T(2,128)S(1)} %get-tuple-element.29), channel_id=1, source_target_pairs={{1,0},{2,1},{3,2},{4,3},{5,4},{6,5},{7,6},{8,7},{9,8},{10,9},{11,1... | collective-permute-start | bytes 30728 | tf_op jit(solution)/shard_map/ppermute | solution.py:17
  407.0 7.4 %copy-start.4 = (f32[27,32,32]{2,1,0:T(8,128)S(1)}, f32[27,32,32]{2,1,0:T(8,128)}, u32[]{:S(2)}) copy-start(f32[27,32,32]{2,1,0:T(8,128)} %param.12) | copy-start | bytes 331780
  408.1 7.3 %collective-permute-start.4 = (f32[32,8,1,128]{3,0,2,1:T(8,128)S(1)}, f32[32,8,1,128]{3,0,2,1:T(8,128)S(1)}, u32[]{:S(2)}, u32[]{:S(2)}) collective-permute-start(f32[32,8,1,128]{3,0,2,1:T(8,128)S(1)} %get-tuple-element.22), channel_id=1, source_target_pairs={{0,16},{16,32},{32,48},{48,64},{64,80},{80,96},{96,112},{112,128},... | collective-permute-start | bytes 393224 | tf_op jit(solution)/shard_map/ppermute | solution.py:16
  410.9 8.9 %collective-permute-start.5 = (f32[32,8,1,128]{3,0,2,1:T(8,128)S(1)}, f32[32,8,1,128]{3,0,2,1:T(8,128)S(1)}, u32[]{:S(2)}, u32[]{:S(2)}) collective-permute-start(f32[32,8,1,128]{3,0,2,1:T(8,128)S(1)} %get-tuple-element.23), channel_id=1, source_target_pairs={{16,0},{32,16},{48,32},{64,48},{80,64},{96,80},{112,96},{128,112},... | collective-permute-start | bytes 393224 | tf_op jit(solution)/shard_map/ppermute | solution.py:17
  419.9 8.8 %collective-permute-start.6 = (f32[32,1,10,128]{3,0,2,1:T(8,128)S(1)}, f32[32,1,10,128]{3,0,2,1:T(8,128)S(1)}, u32[]{:S(2)}, u32[]{:S(2)}) collective-permute-start(f32[32,1,10,128]{3,0,2,1:T(8,128)S(1)} %get-tuple-element.18), channel_id=1, source_target_pairs={{0,1},{1,2},{2,3},{3,4},{4,5},{5,6},{6,7},{7,8},{8,9},{9,10},{10,1... | collective-permute-start | bytes 491528 | tf_op jit(solution)/shard_map/ppermute | solution.py:16
  421.8 10.7 %collective-permute-start.7 = (f32[32,1,10,128]{3,0,2,1:T(8,128)S(1)}, f32[32,1,10,128]{3,0,2,1:T(8,128)S(1)}, u32[]{:S(2)}, u32[]{:S(2)}) collective-permute-start(f32[32,1,10,128]{3,0,2,1:T(8,128)S(1)} %get-tuple-element.19), channel_id=1, source_target_pairs={{1,0},{2,1},{3,2},{4,3},{5,4},{6,5},{7,6},{8,7},{9,8},{10,9},{11,1... | collective-permute-start | bytes 491528 | tf_op jit(solution)/shard_map/ppermute | solution.py:17
  460.4 6.1 %copy-start.7 = (f32[27,2,32]{2,1,0:T(2,128)S(1)}, f32[27,2,32]{2,1,0:T(2,128)}, u32[]{:S(2)}) copy-start(f32[27,2,32]{2,1,0:T(2,128)} %param.13) | copy-start | bytes 20740
  462.1 5.0 collective-permute-start.8
  464.1 7.2 %collective-permute-start.9 = (f32[32,8,1,128]{3,0,2,1:T(8,128)S(1)}, f32[32,8,1,128]{3,0,2,1:T(8,128)S(1)}, u32[]{:S(2)}, u32[]{:S(2)}) collective-permute-start(f32[32,8,1,128]{3,0,2,1:T(8,128)S(1)} %get-tuple-element.21), channel_id=1, source_target_pairs={{16,0},{32,16},{48,32},{64,48},{80,64},{96,80},{112,96},{128,112},... | collective-permute-start | bytes 393224 | tf_op jit(solution)/shard_map/ppermute | solution.py:17
  471.3 8.7 %collective-permute-start.10 = (f32[32,1,10,128]{3,0,2,1:T(8,128)S(1)}, f32[32,1,10,128]{3,0,2,1:T(8,128)S(1)}, u32[]{:S(2)}, u32[]{:S(2)}) collective-permute-start(f32[32,1,10,128]{3,0,2,1:T(8,128)S(1)} %get-tuple-element.16), channel_id=1, source_target_pairs={{0,1},{1,2},{2,3},{3,4},{4,5},{5,6},{6,7},{7,8},{8,9},{9,10},{10,1... | collective-permute-start | bytes 491528 | tf_op jit(solution)/shard_map/ppermute | solution.py:16
  474.8 11.6 %collective-permute-start.11 = (f32[32,1,10,128]{3,0,2,1:T(8,128)S(1)}, f32[32,1,10,128]{3,0,2,1:T(8,128)S(1)}, u32[]{:S(2)}, u32[]{:S(2)}) collective-permute-start(f32[32,1,10,128]{3,0,2,1:T(8,128)S(1)} %get-tuple-element.17), channel_id=1, source_target_pairs={{1,0},{2,1},{3,2},{4,3},{5,4},{6,5},{7,6},{8,7},{9,8},{10,9},{11,1... | collective-permute-start | bytes 491528 | tf_op jit(solution)/shard_map/ppermute | solution.py:17
Sparse Core Ops, SparseCore 0:
  9.8 38.4 all-gather.1
  236.9 119.8 all-reduce.4
where the time goes:
time: 523 us; the launch traced here: 514 us
  waiting for transfers between devices  230 us (44%)
  matrix products  135 us (26%)
  blocking collectives  55.5 us (11%)
  starting transfers between devices  45 us (9%)
  local copies, waits for them, and re-layouts  25.2 us (5%)
  between operations  15.6 us (3%)
  other arithmetic  7.86 us (2%)
    psum x1, waiting for transfers between devices, body(): summed = lax.psum(partial_value, 'coil')  120 us
    dot_general x81, matrix products, conv_valid(): jnp.einsum('oc,czxy->ozxy', weights[offset], window, precision=lax.Precis...  78.9 us
    dot_general x24, matrix products, apply_table(): return jnp.einsum(formula, table, values, precision=lax.Precision.HIGHEST)  55.7 us
    all_to_all x1, blocking collectives, body(): lax.all_to_all(corrected, 'slab', split_axis=2, concat_axis=3, tiled=True)  55.5 us
    all_to_all x1, waiting for transfers between devices, body(): lax.all_to_all(stacked, 'slab', split_axis=3, concat_axis=2, tiled=True)  42 us
    all_gather x1, waiting for transfers between devices, body(): slab_image = lax.all_gather(estimate, 'coil', axis=2, tiled=True)  40.4 us
    ppermute x6, waiting for transfers between devices, padded_2(): after = lax.ppermute(first, axis, down)  26.6 us
    ppermute x6, starting transfers between devices, padded_2(): after = lax.ppermute(first, axis, down)  18.5 us
  transfers between devices with their start and end apart: 15, of which 10 were waited for; matrix products, arithmetic and copies ran while one was open for 3% of the time, Pallas kernels for 0%

commit v1 on v0

v1 whole, which is shorter than its diff:
```python
import math

import jax
import jax.numpy as jnp
import ml_dtypes
import numpy as np
from jax import lax
from jax.experimental import pallas as pl
from jax.experimental.pallas import tpu as pltpu
from jax.sharding import PartitionSpec as P

MESH = pl.DeviceIdType.MESH
F32 = jnp.float32
BF16 = jnp.bfloat16
N = 128
B = 8
G = 16


def tables():
    k = np.arange(N)
    angle = 2.0 * math.pi * (np.outer(k, k) % N) / N
    c, s = np.cos(angle) / math.sqrt(N), np.sin(angle) / math.sqrt(N)
    fwd = np.block([[c, s], [-s, c]])
    inv = np.block([[c, -s], [s, c]])

    def pieces(m):
        hi = m.astype(np.float32).astype(ml_dtypes.bfloat16)
        lo = (m - hi.astype(np.float64)).astype(np.float32).astype(ml_dtypes.bfloat16)
        return [hi, hi, lo]

    return [
        np.concatenate(pieces(fwd), 1),
        np.concatenate(pieces(inv), 1),
        np.concatenate(pieces(inv), 0),
        np.concatenate(pieces(fwd), 0),
    ]


def split(x):
    hi = x.astype(BF16)
    lo = (x - hi.astype(F32)).astype(BF16)
    return hi, lo


def left(table, x):
    hi, lo = split(x)
    return jnp.dot(table, jnp.concatenate([hi, lo, hi], 0), preferred_element_type=F32)


def right(x, table):
    hi, lo = split(x)
    return jnp.dot(jnp.concatenate([hi, lo, hi], 1), table, preferred_element_type=F32)


def loop(count, fn):
    def step(i, carry):
        fn(i)
        return carry

    lax.fori_loop(0, count, step, 0)


def recon_kernel(
    est, maps, meas, weight, lf, li, rf, ri_,
    out,
    gath, send1, recv1, send2, recv2, part, rs_a, rs_b,
    ag_send, ag_recv, a1_send, a1_recv, a2_send, a2_recv, own_sem, rs_send, rs_recv,
):
    me_c = lax.axis_index("coil")
    me_s = lax.axis_index("slab")
    core = lax.rem(me_c, 2)
    chip = me_c // 2
    sibling = me_c + 1 - 2 * core

    barrier = pltpu.get_barrier_semaphore()

    def greet(k):
        pl.semaphore_signal(barrier, inc=1, device_id={"coil": lax.rem(me_c + k + 1, G)}, device_id_type=MESH)
        pl.semaphore_signal(barrier, inc=1, device_id={"slab": lax.rem(me_s + k + 1, G)}, device_id_type=MESH)

    loop(G - 1, greet)
    pl.semaphore_wait(barrier, 2 * (G - 1))

    def ag_copy(src, slot, send_i, target):
        return pltpu.make_async_remote_copy(
            src_ref=src, dst_ref=gath.at[slot], send_sem=ag_send.at[send_i], recv_sem=ag_recv.at[slot],
            device_id={"coil": target}, device_id_type=MESH)

    ag_copy(est, me_c, 0, sibling).start()

    def ag_out(k):
        ag_copy(est, me_c, 1 + k, 2 * lax.rem(chip + k + 1, 8) + core).start()

    loop(7, ag_out)
    gath[me_c] = est[...]

    def ag_in(k):
        slot = 2 * lax.rem(chip + 7 - k, 8) + core
        ag_copy(est, slot, 0, sibling).wait_recv()
        ag_copy(gath.at[slot], slot, 8 + k, sibling).start()

    loop(7, ag_in)

    def ag_last(k):
        slot = 2 * lax.rem(chip + 8 - k, 8) + 1 - core
        ag_copy(est, slot, 0, sibling).wait_recv()

    loop(8, ag_last)

    def a1_copy(c, h, peer, slot):
        return pltpu.make_async_remote_copy(
            src_ref=send1.at[c, :, pl.ds(pl.multiple_of(peer * 64 + h * 32, 32), 32), :],
            dst_ref=recv1.at[c, h, slot],
            send_sem=a1_send.at[2 * c + h, peer], recv_sem=a1_recv.at[2 * c + h, slot],
            device_id={"slab": peer}, device_id_type=MESH)

    def a1_own(c, h):
        return pltpu.make_async_copy(
            send1.at[c, :, pl.ds(pl.multiple_of(me_s * 64 + h * 32, 32), 32), :],
            recv1.at[c, h, me_s], own_sem.at[2 * c + h])

    for c in range(2):
        def fx(zp):
            cols = []
            for j in range(2):
                z = 2 * zp + j
                ir = gath[:, 0, z].reshape(N, N)
                ii = gath[:, 1, z].reshape(N, N)
                mr = maps[c, 0, z]
                mi = maps[c, 1, z]
                cols.append(jnp.concatenate([mr * ir - mi * ii, mr * ii + mi * ir], 0))
            y = left(lf[...], jnp.concatenate(cols, 1))
            for j in range(2):
                for r in range(2):
                    send1[c, r, pl.ds(2 * zp + j, N, stride=B), :] = y[r * N:(r + 1) * N, j * N:(j + 1) * N]

        loop(4, fx)
        for h in range(2):
            def a1_out(k):
                peer = lax.rem(me_s + k + 1, G)
                a1_copy(c, h, peer, me_s).start()

            loop(G - 1, a1_out)
            a1_own(c, h).start()

    def a2_copy(c, h, peer, slot):
        return pltpu.make_async_remote_copy(
            src_ref=send2.at[c, h, peer],
            dst_ref=recv2.at[c, :, pl.ds(pl.multiple_of(slot * 64 + h * 32, 32), 32), :],
            send_sem=a2_send.at[2 * c + h, peer], recv_sem=a2_recv.at[2 * c + h, slot],
            device_id={"slab": peer}, device_id_type=MESH)

    def a2_own(c, h):
        return pltpu.make_async_copy(
            send2.at[c, h, me_s],
            recv2.at[c, :, pl.ds(pl.multiple_of(me_s * 64 + h * 32, 32), 32), :], own_sem.at[4 + 2 * c + h])

    def pencil_chunk(q):
        c = q // 2
        h = lax.rem(q, 2)

        def a1_in(k):
            peer = lax.rem(me_s + G - 1 - k, G)
            a1_copy(c, h, me_s, peer).wait_recv()

        a1_own(c, h).wait()
        loop(G - 1, a1_in)

        def pair(kp):
            rows = []
            for j in range(2):
                at = pl.ds(pl.multiple_of((2 * kp + j) * B, B), B)
                rows.append(jnp.concatenate(
                    [recv1[c, h, :, 0, at, :].reshape(N, N), recv1[c, h, :, 1, at, :].reshape(N, N)], 1))
            y = right(jnp.concatenate(rows, 0), rf[...])
            x = jnp.concatenate([
                jnp.concatenate([y[:N, :N], y[N:, :N]], 1),
                jnp.concatenate([y[:N, N:], y[N:, N:]], 1)], 0)
            x = left(lf[...], x)
            w = weight[...]
            halves = []
            for r in range(2):
                pieces = []
                for j in range(2):
                    k = x[r * N:(r + 1) * N, j * N:(j + 1) * N]
                    m = meas[c, r, pl.ds(h * 4 + 2 * kp + j, N, stride=B), :]
                    pieces.append(k - w * (k - m))
                halves.append(jnp.concatenate(pieces, 1))
            x = left(li[...], jnp.concatenate(halves, 0))
            y = jnp.concatenate([
                jnp.concatenate([x[:N, :N], x[N:, :N]], 1),
                jnp.concatenate([x[:N, N:], x[N:, N:]], 1)], 0)
            y = right(y, ri_[...])
            for j in range(2):
                for r in range(2):
                    send2[c, h, :, r, pl.ds(pl.multiple_of((2 * kp + j) * B, B), B), :] = (
                        y[j * N:(j + 1) * N, r * N:(r + 1) * N].reshape(G, B, N))

        loop(2, pair)

        def a2_out(k):
            peer = lax.rem(me_s + k + 1, G)
            a2_copy(c, h, peer, me_s).start()

        loop(G - 1, a2_out)
        a2_own(c, h).start()

    loop(4, pencil_chunk)

    for c in range(2):
        for h in range(2):
            def a2_in(k):
                peer = lax.rem(me_s + G - 1 - k, G)
                a2_copy(c, h, me_s, peer).wait_recv()

            a2_own(c, h).wait()
            loop(G - 1, a2_in)

        def fx_back(zp):
            cols = []
            for j in range(2):
                at = pl.ds(2 * zp + j, N, stride=B)
                cols.append(jnp.concatenate([recv2[c, 0, at, :], recv2[c, 1, at, :]], 0))
            x = left(li[...], jnp.concatenate(cols, 1))
            for j in range(2):
                z = 2 * zp + j
                br = x[:N, j * N:(j + 1) * N]
                bi = x[N:, j * N:(j + 1) * N]
                mr = maps[c, 0, z]
                mi = maps[c, 1, z]
                pr = (mr * br + mi * bi).reshape(8, 2, B, N)
                pi = (mr * bi - mi * br).reshape(8, 2, B, N)
                for g in range(2):
                    if c == 0:
                        part[g, :, 0, z] = pr[:, g]
                        part[g, :, 1, z] = pi[:, g]
                    else:
                        part[g, :, 0, z] = part[g, :, 0, z] + pr[:, g]
                        part[g, :, 1, z] = part[g, :, 1, z] + pi[:, g]

        loop(4, fx_back)

    to_sibling = pltpu.make_async_remote_copy(
        src_ref=part.at[1 - core], dst_ref=rs_a, send_sem=rs_send.at[8], recv_sem=rs_recv.at[8],
        device_id={"coil": sibling}, device_id_type=MESH)
    to_sibling.start()
    to_sibling.wait_recv()

    def rs_copy(target, slot):
        return pltpu.make_async_remote_copy(
            src_ref=rs_a.at[target], dst_ref=rs_b.at[slot], send_sem=rs_send.at[target], recv_sem=rs_recv.at[slot],
            device_id={"coil": 2 * target + core}, device_id_type=MESH)

    def rs_out(k):
        target = lax.rem(chip + k + 1, 8)
        rs_a[target] = rs_a[target] + part[core, target]
        rs_copy(target, chip).start()

    loop(7, rs_out)
    out[...] = rs_a[chip] + part[core, chip]

    def rs_in(k):
        slot = lax.rem(chip + 7 - k, 8)
        rs_copy(chip, slot).wait_recv()
        out[...] = out[...] + rs_b[slot]

    loop(7, rs_in)

    to_sibling.wait_send()

    def drain_small(k):
        rs_copy(lax.rem(chip + k + 1, 8), chip).wait_send()

    loop(7, drain_small)

    def drain_ag(k):
        ag_copy(est, me_c, k, sibling).wait_send()

    loop(15, drain_ag)

    def drain_a2a(i):
        q = i // (G - 1)
        peer = lax.rem(me_s + lax.rem(i, G - 1) + 1, G)
        a1_copy(q // 2, lax.rem(q, 2), peer, me_s).wait_send()
        a2_copy(q // 2, lax.rem(q, 2), peer, me_s).wait_send()

    loop(4 * (G - 1), drain_a2a)


def recon(estimate, coil_maps, measured, weight, tabs):
    measured = measured.reshape(2, 2, N * B, N)
    vmem = pl.BlockSpec(memory_space=pltpu.VMEM)
    dma = pltpu.SemaphoreType.DMA
    return pl.pallas_call(
        recon_kernel,
        out_shape=jax.ShapeDtypeStruct((2, B, B, N), F32),
        in_specs=[vmem] * 8,
        out_specs=vmem,
        scratch_shapes=[
            pltpu.VMEM((G, 2, B, B, N), F32),
            pltpu.VMEM((2, 2, N * B, N), F32),
            pltpu.VMEM((2, 2, G, 2, 32, N), F32),
            pltpu.VMEM((2, 2, G, 2, 32, N), F32),
            pltpu.VMEM((2, 2, N * B, N), F32),
            pltpu.VMEM((2, 8, 2, B, B, N), F32),
            pltpu.VMEM((8, 2, B, B, N), F32),
            pltpu.VMEM((8, 2, B, B, N), F32),
            dma((15,)), dma((G,)), dma((4, G)), dma((4, G)), dma((4, G)), dma((4, G)), dma((8,)), dma((9,)), dma((9,)),
        ],
        compiler_params=pltpu.CompilerParams(
            collective_id=0, has_side_effects=True, vmem_limit_bytes=48 * 2**20),
    )(estimate, coil_maps, measured, weight, *tabs)


def conv_weights(w_first, w_middle, w_last):
    def select(outs, ins, shift):
        x, d, i = np.ogrid[:outs, :3, :ins]
        return jnp.asarray((i - shift == x + d).astype(np.float32))

    def pieces(w, axis):
        hi = lax.reduce_precision(w, 8, 7)
        return jnp.stack([hi, hi, w - hi], axis).astype(BF16)

    hp = lax.Precision.HIGHEST
    w1 = jnp.einsum("zxyoc,pxq->ypozcq", w_first.reshape(3, 3, 3, 32, 2), select(12, 24, 5), precision=hp)
    w1 = pieces(w1.reshape(1152, 3, 48), 2).reshape(1152, 432)
    w2 = jnp.einsum("zxyoc,pxq->ypozqc", w_middle.reshape(3, 3, 3, 32, 32), select(5, 8, 0), precision=hp)
    w2 = pieces(w2.reshape(480, 3, 256), 2).reshape(480, 2304)
    w3 = jnp.einsum("zxyoc,pxq->zyopqc", w_last.reshape(3, 3, 3, 2, 32), select(8, 10, 0), precision=hp)
    w3 = pieces(w3.reshape(144, 320), 1).reshape(144, 960)
    return w1, w2, w3


def shifted_sum(p0, p1, p2):
    lane = lax.broadcasted_iota(jnp.int32, p0.shape, 1)
    down = jnp.where(lane == 0, 0.0, pltpu.roll(p0, 1, 1))
    up = jnp.where(lane == N - 1, 0.0, pltpu.roll(p2, N - 1, 1))
    return p1 + down + up


def denoise_kernel(comb, w1, w2, w3, refined, big, f0h, f0l, f1h, f1l, f2h, f2l, q3, send_sem, recv_sem):
    me_c = lax.axis_index("coil")
    me_s = lax.axis_index("slab")
    barrier = pltpu.get_barrier_semaphore()
    near = [(a, b) for a in (-1, 0, 1) for b in (-1, 0, 1) if (a, b) != (0, 0)]

    def target(dz, dx):
        return {"coil": lax.rem(me_c + dx + G, G), "slab": lax.rem(me_s + dz + G, G)}

    for dz, dx in near:
        pl.semaphore_signal(barrier, inc=1, device_id=target(dz, dx), device_id_type=MESH)
    pl.semaphore_wait(barrier, 8)

    source = {-1: (0, 3), 0: (0, 8), 1: (5, 3)}
    place = {-1: (11, 3), 0: (3, 8), 1: (0, 3)}
    copies = []
    for i, (dz, dx) in enumerate(near):
        a, n = source[dz]
        b, n = place[dz]
        copies.append(pltpu.make_async_remote_copy(
            src_ref=comb.at[:, pl.ds(a, n)], dst_ref=big.at[1 - dx, :, pl.ds(b, n)],
            send_sem=send_sem.at[i], recv_sem=recv_sem.at[i],
            device_id=target(dz, dx), device_id_type=MESH))
        copies[-1].start()
    big[1, :, 3:11] = comb[...]
    f1h[384:, :] = jnp.zeros((32, 12 * N), BF16)
    f1l[384:, :] = jnp.zeros((32, 12 * N), BF16)
    for copy in copies:
        copy.wait_recv()

    for z in range(14):
        rows = []
        for c in range(2):
            for blk in range(3):
                v = big[blk, c, z]
                if blk == 0:
                    v = jnp.where(me_c == 0, 0.0, v)
                if blk == 2:
                    v = jnp.where(me_c == G - 1, 0.0, v)
                if z < 3:
                    v = jnp.where(me_s == 0, 0.0, v)
                if z >= 11:
                    v = jnp.where(me_s == G - 1, 0.0, v)
                rows.append(v)
        hi, lo = split(jnp.concatenate(rows, 0))
        f0h[:, z * N:(z + 1) * N] = hi
        f0l[:, z * N:(z + 1) * N] = lo

    def inside(rows, first_x, z):
        x = me_c * B + first_x + lax.broadcasted_iota(jnp.int32, (rows, N), 0) // 32
        z = me_s * B + z
        return (x >= 0) & (x < N) & (z >= 0) & (z < N)

    def conv1(i):
        parts = []
        for dz in range(3):
            at = pl.ds(pl.multiple_of((2 * i + dz) * N, N), 2 * N)
            hi = f0h[:, at]
            parts += [hi, f0l[:, at], hi]
        y = jnp.dot(w1[...], jnp.concatenate(parts, 0), preferred_element_type=F32)
        for j in range(2):
            p = [y[d * 384:(d + 1) * 384, j * N:(j + 1) * N] for d in range(3)]
            v = jnp.maximum(shifted_sum(*p), 0.0)
            v = jnp.where(inside(384, -2, 2 * i + j - 2), v, 0.0)
            hi, lo = split(v)
            at = pl.ds(pl.multiple_of((2 * i + j) * N, N), N)
            f1h[0:384, at] = hi
            f1l[0:384, at] = lo

    loop(6, conv1)

    def conv2(i):
        for g in range(2):
            parts = []
            for dz in range(3):
                at = pl.ds(pl.multiple_of((2 * i + dz) * N, N), 2 * N)
                hi = f1h[g * 160:g * 160 + 256, at]
                parts += [hi, f1l[g * 160:g * 160 + 256, at], hi]
            y = jnp.dot(w2[...], jnp.concatenate(parts, 0), preferred_element_type=F32)
            for j in range(2):
                p = [y[d * 160:(d + 1) * 160, j * N:(j + 1) * N] for d in range(3)]
                v = jnp.maximum(shifted_sum(*p), 0.0)
                v = jnp.where(inside(160, g * 5 - 1, 2 * i + j - 1), v, 0.0)
                hi, lo = split(v)
                at = pl.ds(pl.multiple_of((2 * i + j) * N, N), N)
                f2h[g * 160:(g + 1) * 160, at] = hi
                f2l[g * 160:(g + 1) * 160, at] = lo

    loop(5, conv2)

    def conv3(i):
        at = pl.ds(pl.multiple_of(2 * i * N, N), 2 * N)
        hi = f2h[:, at]
        y = jnp.dot(w3[...], jnp.concatenate([hi, f2l[:, at], hi], 0), preferred_element_type=F32)
        q3[2 * i] = y[:, :N]
        q3[2 * i + 1] = y[:, N:]

    loop(5, conv3)

    def last(z):
        p = []
        for dy in range(3):
            p.append(sum(q3[z + dz, dz * 48 + dy * 16:dz * 48 + dy * 16 + 16, :] for dz in range(3)))
        v = shifted_sum(*p)
        refined[0, z] = comb[0, z] + v[:B]
        refined[1, z] = comb[1, z] + v[B:]

    loop(B, last)
    for copy in copies:
        copy.wait_send()


def denoise(combined, w1, w2, w3):
    vmem = pl.BlockSpec(memory_space=pltpu.VMEM)
    dma = pltpu.SemaphoreType.DMA
    return pl.pallas_call(
        denoise_kernel,
        out_shape=jax.ShapeDtypeStruct((2, B, B, N), F32),
        in_specs=[vmem] * 4,
        out_specs=vmem,
        scratch_shapes=[
            pltpu.VMEM((3, 2, 14, B, N), F32),
            pltpu.VMEM((48, 14 * N), BF16), pltpu.VMEM((48, 14 * N), BF16),
            pltpu.VMEM((416, 12 * N), BF16), pltpu.VMEM((416, 12 * N), BF16),
            pltpu.VMEM((320, 10 * N), BF16), pltpu.VMEM((320, 10 * N), BF16),
            pltpu.VMEM((10, 144, N), F32),
            dma((8,)), dma((8,)),
        ],
        compiler_params=pltpu.CompilerParams(
            collective_id=1, has_side_effects=True, vmem_limit_bytes=48 * 2**20),
    )(combined, w1, w2, w3)


def body(estimate, coil_maps, measured, line_mask, w_first, w_middle, w_last):
    tabs = [jnp.asarray(t) for t in tables()]
    weight = (line_mask == 1).astype(F32) * 0.5
    combined = recon(estimate, coil_maps, measured, weight, tabs)
    refined = denoise(combined, *conv_weights(w_first, w_middle, w_last))
    return combined, refined


def solution(mesh):
    in_specs = (
        P(None, "slab", "coil", None),
        P("coil", None, "slab", None, None),
        P("coil", None, None, "slab", None),
        P(),
        P(),
        P(),
        P(),
    )
    out_specs = (P(None, "slab", "coil", None), P(None, "slab", "coil", None))
    return jax.shard_map(body, mesh=mesh, in_specs=in_specs, out_specs=out_specs, check_vma=False)
```

time: 523 us -> 201 us (0.38)
  the two profiles are of different devices: /device:TPU:103 before, /device:TPU:1 now
where the time goes in v1:
time: 201 us; the launch traced here: 200 us
  Pallas kernels  153 us (76%)
  local copies, waits for them, and re-layouts  35.1 us (17%)
  matrix products  9.55 us (5%)
    pallas_call x1, Pallas kernels, recon(): pl.pallas_call(recon_kernel, out_shape=jax.ShapeDtypeStruct((2, B, B, N),...  129 us
    pallas_call x1, Pallas kernels, denoise(): pl.pallas_call(denoise_kernel, out_shape=jax.ShapeDtypeStruct((2, B, B, N...  23.5 us
    unnamed x28, local copies, waits for them, and re-layouts  8.45 us
    convert_element_type x3, local copies, waits for them, and re-layouts, pieces(): return jnp.stack([hi, hi, w - hi], axis).astype(BF16)  6.63 us
    dot_general x1, matrix products, conv_weights(): jnp.einsum('zxyoc,pxq->ypozqc', w_middle.reshape(3, 3, 3, 32, 32), select...  6.1 us
    another operation x3, local copies, waits for them, and re-layouts, pieces(): return jnp.stack([hi, hi, w - hi], axis).astype(BF16)  4.44 us
    reshape x1, local copies, waits for them, and re-layouts, conv_weights(): w2 = pieces(w2.reshape(480, 3, 256), 2).reshape(480, 2304)  4.17 us

profile of v1, /device:TPU:1, one launch (start us, length us, event | category | flops | bytes accessed | tf_op | source)
XLA Modules:
  0.0 200.0 jit_solution(8900433116932995655)
XLA Ops:
  0.6 6.1 %convolution_bitcast_fusion = f32[3,5,32,3,8,32]{5,4,2,0,3,1:T(8,128)S(1)} fusion(f32[5,3,8,1,1,1]{2,1,5,4,3,0:T(4,128)} %constant.31, f32[3,3,3,32,32]{4,3,2,1,0:T(8,128)} %bitcast.42), kind=kOutput, calls=%fused_computation | convolution fusion | flops 13271040 | bytes 1585632 | tf_op jit(solution)/shard_map/zxyoc,pxq->ypozqc/dot_general | solution.py:328
  6.7 2.9 %copy.23 = f32[3,5,32,3,8,32]{5,4,2,1,0,3:T(8,128)} copy(f32[3,5,32,3,8,32]{5,4,2,0,3,1:T(8,128)S(1)} %convolution_bitcast_fusion) | data formatting | bytes 2949120 | tf_op jit(solution)/shard_map/zxyoc,pxq->ypozqc/transpose | solution.py:328
  9.6 4.2 %reshape.107 = f32[480,3,1,256]{3,0,1,2:T(8,128)S(1)} reshape(f32[3,5,32,3,8,32]{5,4,2,1,0,3:T(8,128)} %copy.23) | data formatting | bytes 2949120 | tf_op jit(solution)/shard_map/reshape | solution.py:329
  13.8 0.2 reduce-precision_convert_fusion
  14.1 0.2 pad_maximum_fusion
  14.3 2.5 %copy.24 = bf16[480,3,3,256]{0,3,2,1:T(8,128)(2,1)} copy(bf16[480,3,3,256]{3,0,1,2:T(8,128)(2,1)S(1)} %pad_maximum_fusion) | data formatting | bytes 4423680 | tf_op jit(solution)/shard_map/stack | solution.py:323
  16.8 0.0 copy-start.10
  16.8 0.0 copy-start.11
  16.8 2.8 %copy.29.w2 = bf16[480,2304]{1,0:T(8,128)(2,1)S(1)} copy(bf16[480,2304]{0,1:T(8,128)(2,1)} %bitcast.40) | data formatting | bytes 4423680 | tf_op jit(solution)/shard_map/convert_element_type | solution.py:323
  19.6 0.0 copy-done.10
  19.6 0.0 copy-done.11
  19.6 2.3 %convolution_bitcast_fusion.1 = f32[3,12,32,3,2,24]{2,5,4,0,3,1:T(8,128)S(1)} fusion(f32[12,3,24,1,1,1]{2,1,5,4,3,0:T(4,128)S(1)} %copy-done.11, f32[3,3,3,32,2]{3,4,2,1,0:T(2,128)S(1)} %bitcast.44), kind=kOutput, calls=%fused_computation.4 | convolution fusion | flops 5971968 | bytes 673920 | tf_op jit(solution)/shard_map/zxyoc,pxq->ypozcq/dot_general | solution.py:326
  21.9 2.6 %copy.20 = f32[3,12,32,3,2,24]{2,1,0,5,4,3:T(8,128)} copy(f32[3,12,32,3,2,24]{2,5,4,0,3,1:T(8,128)S(1)} %convolution_bitcast_fusion.1) | data formatting | bytes 1327104 | tf_op jit(solution)/shard_map/zxyoc,pxq->ypozcq/transpose | solution.py:326
  24.5 2.5 %reshape.105 = f32[1152,3,1,48]{0,3,1,2:T(8,128)S(1)} reshape(f32[3,12,32,3,2,24]{2,1,0,5,4,3:T(8,128)} %copy.20) | data formatting | bytes 1327104 | tf_op jit(solution)/shard_map/reshape | solution.py:327
  27.0 0.1 reduce-precision_convert_fusion.1
  27.1 0.1 pad_maximum_fusion.1
  27.3 0.0 copy-start.9
  27.3 0.0 copy-start.12
  27.3 1.0 copy.21
  28.3 1.7 copy.28.w1
  30.1 0.0 copy-done.9
  30.1 0.0 copy-done.12
  30.1 1.2 convolution_bitcast_fusion.2
  31.3 1.2 copy.26
  32.4 0.0 copy-start.8
  32.4 0.0 copy-start.7
  32.4 2.3 %reshape.109 = f32[144,1,320]{2,0,1:T(8,128)} reshape(f32[3,3,2,8,10,32]{5,4,3,2,1,0:T(8,128)} %copy.26) | data formatting | bytes 368640 | tf_op jit(solution)/shard_map/reshape | solution.py:331
  34.7 1.0 reduce-precision_convert_fusion.2
  35.7 0.1 pad_maximum_fusion.2
  35.8 0.9 copy.27
  36.7 2.1 %convert_element_type.18.w3 = bf16[144,960]{1,0:T(8,128)(2,1)} reshape(bf16[144,3,320]{2,1,0:T(4,128)(2,1)} %copy.27) | data formatting | bytes 552960 | tf_op jit(solution)/shard_map/convert_element_type | solution.py:323
  38.8 0.0 copy-done.8
  38.8 0.0 copy-done.7
  38.8 0.0 copy-start
  38.8 1.6 copy-done
  40.4 0.0 copy-start.1
  40.4 1.6 copy-done.1
  42.0 0.0 copy-start.3
  42.0 1.0 copy-done.3
  43.0 0.0 copy-start.4
  43.0 1.0 copy-done.4
  44.0 0.0 copy-start.5
  44.0 1.0 copy-done.5
  45.0 0.0 copy-start.6
  45.0 1.0 copy-done.6
  46.0 0.0 copy-start.2
  46.0 129.3 %shard_map.149.comb = f32[2,8,8,128]{3,2,1,0:T(8,128)S(1)} custom-call(f32[2,8,8,128]{3,2,1,0:T(8,128)S(1)} %copy-done.7, f32[2,2,8,128,128]{4,3,2,1,0:T(8,128)S(1)} %copy-done, f32[2,2,1024,128]{3,2,1,0:T(8,128)S(1)} %bitcast.39, f32[128,128]{1,0:T(8,128)S(1)} %compare_select_fusion.weight, bf16[256,768]{1,0:T(8,128)(2,1)S(1)} %copy-done.3, ...), custom_call_target="tpu_custom_call" | custom-call | tf_op jit(solution)/shard_map/pallas_call | solution.py:295
  175.3 0.0 copy-done.2
  175.3 23.5 %shard_map.150 = f32[2,8,8,128]{3,2,1,0:T(8,128)S(1)} custom-call(f32[2,8,8,128]{3,2,1,0:T(8,128)S(1)} %shard_map.149.comb, bf16[1152,432]{1,0:T(8,128)(2,1)S(1)} %copy.28.w1, bf16[480,2304]{1,0:T(8,128)(2,1)S(1)} %copy.29.w2, bf16[144,960]{1,0:T(8,128)(2,1)S(1)} %copy-done.2), custom_call_target="tpu_custom_call" | custom-call | tf_op jit(solution)/shard_map/pallas_call | solution.py:457
  198.8 0.6 copy.47
  199.4 0.6 copy.48
  (1 shorter events, 0.0 us)
Async XLA Ops:
  16.8 2.8 %copy-start.10 = (f32[27,32,2]{1,2,0:T(2,128)S(1)}, f32[27,32,2]{1,2,0:T(2,128)}, u32[]{:S(2)}) copy-start(f32[27,32,2]{1,2,0:T(2,128)} %param.18) | copy-start | bytes 20740
  16.8 2.8 %copy-start.11 = (f32[12,3,24,1,1,1]{2,1,5,4,3,0:T(4,128)S(1)}, f32[12,3,24,1,1,1]{2,1,5,4,3,0:T(4,128)}, u32[]{:S(2)}) copy-start(f32[12,3,24,1,1,1]{2,1,5,4,3,0:T(4,128)} %constant.30) | copy-start | bytes 10372
  27.3 2.8 %copy-start.9 = (f32[27,2,32]{2,1,0:T(2,128)S(1)}, f32[27,2,32]{2,1,0:T(2,128)}, u32[]{:S(2)}) copy-start(f32[27,2,32]{2,1,0:T(2,128)} %param.20) | copy-start | bytes 20740
  27.3 2.8 %copy-start.12 = (f32[8,3,10,1,1,1]{2,1,5,4,3,0:T(4,128)S(1)}, f32[8,3,10,1,1,1]{2,1,5,4,3,0:T(4,128)}, u32[]{:S(2)}) copy-start(f32[8,3,10,1,1,1]{2,1,5,4,3,0:T(4,128)} %constant.32) | copy-start | bytes 2884
  32.4 6.3 %copy-start.8 = (s32[128,128]{1,0:T(8,128)S(1)}, s32[128,128]{1,0:T(8,128)}, u32[]{:S(2)}) copy-start(s32[128,128]{1,0:T(8,128)} %param.17) | copy-start | bytes 196612
  32.4 6.4 %copy-start.7 = (f32[2,8,8,128]{3,2,1,0:T(8,128)S(1)}, f32[2,8,8,128]{3,2,1,0:T(8,128)}, u32[]{:S(2)}) copy-start(f32[2,8,8,128]{3,2,1,0:T(8,128)} %est.1) | copy-start | bytes 196612
  38.8 1.6 copy-start
  40.4 1.6 copy-start.1
  42.0 1.0 copy-start.3
  43.0 1.0 copy-start.4
  44.0 1.0 copy-start.5
  45.0 1.0 copy-start.6
  46.0 129.3 %copy-start.2 = (bf16[144,960]{1,0:T(8,128)(2,1)S(1)}, bf16[144,960]{1,0:T(8,128)(2,1)}, u32[]{:S(2)}) copy-start(bf16[144,960]{1,0:T(8,128)(2,1)} %convert_element_type.18.w3) | copy-start | bytes 829444

commit v2 on v1

v2 whole, which is shorter than its diff:
```python
import math

import jax
import jax.numpy as jnp
import ml_dtypes
import numpy as np
from jax import lax
from jax.experimental import pallas as pl
from jax.experimental.pallas import tpu as pltpu
from jax.sharding import PartitionSpec as P

MESH = pl.DeviceIdType.MESH
F32 = jnp.float32
BF16 = jnp.bfloat16
N = 128
B = 8
G = 16
Q = 4
ZQ = B // Q
ROWS = B * ZQ
CHUNK = G * ROWS


def tables():
    k = np.arange(N)
    angle = 2.0 * math.pi * (np.outer(k, k) % N) / N
    c, s = np.cos(angle) / math.sqrt(N), np.sin(angle) / math.sqrt(N)
    fwd = np.block([[c, s], [-s, c]])
    inv = np.block([[c, -s], [s, c]])

    def pieces(m):
        hi = m.astype(np.float32).astype(ml_dtypes.bfloat16)
        lo = (m - hi.astype(np.float64)).astype(np.float32).astype(ml_dtypes.bfloat16)
        return [hi, hi, lo]

    one, chunk, slab = np.meshgrid(np.arange(ZQ), np.arange(Q), np.arange(G), indexing="ij")
    order = (slab * B + chunk * ZQ + one).reshape(-1)
    order = np.concatenate([order, order + N])
    return [
        np.concatenate(pieces(fwd), 1),
        np.concatenate(pieces(inv), 1),
        np.concatenate(pieces(inv), 0),
        np.concatenate(pieces(fwd), 0),
        np.concatenate(pieces(fwd[:, order]), 1),
        np.concatenate(pieces(inv[order]), 1),
    ]


def split(x):
    hi = x.astype(BF16)
    lo = (x - hi.astype(F32)).astype(BF16)
    return hi, lo


def left(table, x):
    hi, lo = split(x)
    return jnp.dot(table, jnp.concatenate([hi, lo, hi], 0), preferred_element_type=F32)


def right(x, table):
    hi, lo = split(x)
    return jnp.dot(jnp.concatenate([hi, lo, hi], 1), table, preferred_element_type=F32)


def loop(count, fn):
    def step(i, carry):
        fn(i)
        return carry

    lax.fori_loop(0, count, step, 0)


def shifted_sum(p0, p1, p2):
    lane = lax.broadcasted_iota(jnp.int32, p0.shape, 1)
    down = jnp.where(lane == 0, 0.0, pltpu.roll(p0, 1, 1))
    up = jnp.where(lane == N - 1, 0.0, pltpu.roll(p2, N - 1, 1))
    return p1 + down + up


def build_weights(wf, wm, wl, w1, w2, w3):
    lane = lax.broadcasted_iota(jnp.int32, (32, 512), 1)
    for dy in range(3):
        base = jnp.zeros((32, 512), F32)
        for dz in range(3):
            for dx in range(3):
                taps = wf[dz * 9 + dx * 3 + dy]
                for c in range(2):
                    base = jnp.where(lane == dz * 48 + c * 24 + dx + 5, taps[:, c:c + 1], base)
        hi = base.astype(BF16).astype(F32)
        full = hi + pltpu.roll(hi, 144, 1) + pltpu.roll(base - hi, 288, 1)
        for xo in range(12):
            r = (dy * 12 + xo) * 32
            w1[r:r + 32, :] = (pltpu.roll(full, xo, 1) if xo else full).astype(BF16)
    for dz in range(3):
        for dy in range(3):
            base = jnp.concatenate(
                [wm[dz * 9 + dx * 3 + dy] for dx in range(3)] + [jnp.zeros((32, 160), F32)], 1)
            for xo in range(5):
                hi, lo = split(pltpu.roll(base, 32 * xo, 1) if xo else base)
                r = (dy * 5 + xo) * 32
                w2[r:r + 32, dz * 768:dz * 768 + 256] = hi
                w2[r:r + 32, dz * 768 + 256:dz * 768 + 512] = hi
                w2[r:r + 32, dz * 768 + 512:dz * 768 + 768] = lo
    for dz in range(3):
        for dy in range(3):
            base = jnp.concatenate(
                [wl[dz * 9 + dx * 3 + dy] for dx in range(3)] + [jnp.zeros((2, 416), F32)], 1)
            both = jnp.concatenate([jnp.broadcast_to(base[o:o + 1], (8, 512)) for o in range(2)], 0)
            row = lax.broadcasted_iota(jnp.int32, (16, 512), 0) % 8
            moved = both
            for xo in range(1, 8):
                moved = jnp.where(row == xo, pltpu.roll(both, 32 * xo, 1), moved)
            hi, lo = split(moved[:, :384])
            r = dz * 48 + dy * 16
            w3[r:r + 16, :] = hi
            w3[144 + r:160 + r, :] = lo


def kernel(
    est_in, maps_in, meas_in, mask_in, wf_in, wm_in, wl_in, t0, t1, t2, t3, t4, t5,
    combined, refined,
    est, maps, meas, mask, wf, wm, wl, lf, li, rf, ri_, lzf, lzi,
    gath, send1, recv1, send2, recv2, part, rs_a, rs_b,
    w1, w2, w3, big, f0h, f0l, f1h, f1l, f2h, f2l, q3,
    load_sem, ag_send, ag_recv, a1_send, a1_recv, a2_send, a2_recv,
    sib_send, sib_recv, rs_send, rs_recv, halo_send, halo_recv,
):
    me_c = lax.axis_index("coil")
    me_s = lax.axis_index("slab")
    core = lax.rem(me_c, 2)
    chip = me_c // 2
    sibling = me_c + 1 - 2 * core

    barrier = pltpu.get_barrier_semaphore()

    def near_id(dz, dx):
        return {"coil": lax.rem(me_c + dx + G, G), "slab": lax.rem(me_s + dz + G, G)}

    def greet(k):
        pl.semaphore_signal(barrier, inc=1, device_id={"coil": lax.rem(me_c + k + 1, G)}, device_id_type=MESH)
        pl.semaphore_signal(barrier, inc=1, device_id={"slab": lax.rem(me_s + k + 1, G)}, device_id_type=MESH)

    loop(G - 1, greet)
    for dz in (-1, 1):
        for dx in (-1, 1):
            pl.semaphore_signal(barrier, inc=1, device_id=near_id(dz, dx), device_id_type=MESH)

    pairs = [(est_in, est), (t0, lf), (maps_in, maps), (wf_in, wf), (wm_in, wm), (wl_in, wl), (t2, rf), (t4, lzf),
             (meas_in, meas), (mask_in, mask), (t5, lzi), (t3, ri_), (t1, li)]
    loads = [pltpu.make_async_copy(a, b, load_sem.at[i]) for i, (a, b) in enumerate(pairs)]
    for load in loads:
        load.start()
    pl.semaphore_wait(barrier, 2 * (G - 1) + 4)

    def ag_copy(src, q, slot, target):
        return pltpu.make_async_remote_copy(
            src_ref=src, dst_ref=gath.at[q, slot], send_sem=ag_send, recv_sem=ag_recv.at[q, slot],
            device_id={"coil": target}, device_id_type=MESH)

    loads[0].wait()
    for q in range(Q):
        mine = est.at[:, pl.ds(q * ZQ, ZQ)]

        def ag_out(k):
            ag_copy(mine, q, me_c, 2 * lax.rem(chip + k + 1, 8) + core).start()

        loop(7, ag_out)
        ag_copy(mine, q, me_c, sibling).start()
        gath[q, me_c] = est[:, q * ZQ:(q + 1) * ZQ]

    def forward(q):
        def ag_in(k):
            slot = 2 * lax.rem(chip + 7 - k, 8) + core
            ag_copy(gath.at[q, slot], q, slot, sibling).wait_recv()
            ag_copy(gath.at[q, slot], q, slot, sibling).start()

        loop(7, ag_in)

    def exchange(buf, dst, c, q, peer, slot, send_sem, recv_sem):
        return pltpu.make_async_remote_copy(
            src_ref=buf.at[c, :, pl.ds(pl.multiple_of(q * CHUNK + peer * ROWS, ROWS), ROWS), :],
            dst_ref=dst.at[c, :, pl.ds(pl.multiple_of(q * CHUNK + slot * ROWS, ROWS), ROWS), :],
            send_sem=send_sem, recv_sem=recv_sem.at[c, q],
            device_id={"slab": peer}, device_id_type=MESH)

    def exchange_out(buf, dst, c, q, send_sem, recv_sem):
        def out(k):
            exchange(buf, dst, c, q, lax.rem(me_s + k + 1, G), me_s, send_sem, recv_sem).start()

        loop(G - 1, out)
        own = pl.ds(pl.multiple_of(q * CHUNK + me_s * ROWS, ROWS), ROWS)
        for r in range(2):
            dst[c, r, own, :] = buf[c, r, own, :]

    def all_of(buf, c, q):
        return buf.at[c, :, pl.ds(pl.multiple_of(q * CHUNK, CHUNK), CHUNK - ROWS), :]

    def exchange_in(dst, c, q, recv_sem):
        ref = all_of(dst, c, q)
        pltpu.make_async_copy(ref, ref, recv_sem.at[c, q]).wait()

    def slab_chunk(c, q):
        cols = []
        for j in range(ZQ):
            z = q * ZQ + j
            ir = gath[q, :, 0, j].reshape(N, N)
            ii = gath[q, :, 1, j].reshape(N, N)
            mr = maps[c, 0, z]
            mi = maps[c, 1, z]
            cols.append(jnp.concatenate([mr * ir - mi * ii, mr * ii + mi * ir], 0))
        y = left(lf[...], jnp.concatenate(cols, 1))
        for j in range(ZQ):
            for r in range(2):
                send1[c, r, pl.ds(q * CHUNK + j, N, stride=ZQ), :] = y[r * N:(r + 1) * N, j * N:(j + 1) * N]
        exchange_out(send1, recv1, c, q, a1_send, a1_recv)

    forward(0)
    for q in range(Q):
        def ag_last(k):
            slot = 2 * lax.rem(chip + 8 - k, 8) + 1 - core
            ag_copy(gath.at[q, slot], q, slot, sibling).wait_recv()

        loop(8, ag_last)
        if q == 0:
            loads[1].wait()
            loads[2].wait()
        slab_chunk(0, q)
        if q + 1 < Q:
            forward(q + 1)
    loop(Q, lambda q: slab_chunk(1, q))

    for load in loads[3:]:
        load.wait()
    build_weights(wf, wm, wl, w1, w2, w3)
    f1h[384:, :] = jnp.zeros((32, 12 * N), BF16)
    f1l[384:, :] = jnp.zeros((32, 12 * N), BF16)

    def pencils(c):
        loop(Q, lambda q: exchange_in(recv1, c, q, a1_recv))

        def pair(kp):
            rows = []
            for j in range(2):
                halves = []
                for r in range(2):
                    halves.append(jnp.concatenate([
                        recv1[c, r, pl.ds((2 * kp + j) * ZQ + i, Q * G, stride=ROWS), :] for i in range(ZQ)], 0))
                rows.append(jnp.concatenate(halves, 1))
            y = right(jnp.concatenate(rows, 0), rf[...])
            x = jnp.concatenate([
                jnp.concatenate([y[:N, :N], y[N:, :N]], 1),
                jnp.concatenate([y[:N, N:], y[N:, N:]], 1)], 0)
            x = left(lzf[...], x)
            w = jnp.where(mask[...] == 1, 0.5, 0.0)
            halves = []
            for r in range(2):
                pieces = []
                for j in range(2):
                    k = x[r * N:(r + 1) * N, j * N:(j + 1) * N]
                    m = meas[c, r, pl.ds(2 * kp + j, N, stride=B), :]
                    pieces.append(k - w * (k - m))
                halves.append(jnp.concatenate(pieces, 1))
            x = left(lzi[...], jnp.concatenate(halves, 0))
            y = jnp.concatenate([
                jnp.concatenate([x[:N, :N], x[N:, :N]], 1),
                jnp.concatenate([x[:N, N:], x[N:, N:]], 1)], 0)
            y = right(y, ri_[...])
            for j in range(2):
                for r in range(2):
                    for i in range(ZQ):
                        send2[c, r, pl.ds((2 * kp + j) * ZQ + i, Q * G, stride=ROWS), :] = (
                            y[j * N + i * Q * G:j * N + (i + 1) * Q * G, r * N:(r + 1) * N])

        loop(4, pair)
        loop(Q, lambda p: exchange_out(send2, recv2, c, p, a2_send, a2_recv))

    loop(2, pencils)

    def to_sibling(p):
        return pltpu.make_async_remote_copy(
            src_ref=part.at[p, 1 - core], dst_ref=rs_a.at[p], send_sem=sib_send, recv_sem=sib_recv.at[p],
            device_id={"coil": sibling}, device_id_type=MESH)

    def rs_copy(p, target, slot):
        return pltpu.make_async_remote_copy(
            src_ref=rs_a.at[p, target], dst_ref=rs_b.at[p, slot], send_sem=rs_send, recv_sem=rs_recv.at[p],
            device_id={"coil": 2 * target + core}, device_id_type=MESH)

    def finish(p):
        exchange_in(recv2, 0, p, a2_recv)
        exchange_in(recv2, 1, p, a2_recv)
        sums = [[None, None] for j in range(ZQ)]
        for c in range(2):
            cols = []
            for j in range(ZQ):
                at = pl.ds(p * CHUNK + j, N, stride=ZQ)
                cols.append(jnp.concatenate([recv2[c, 0, at, :], recv2[c, 1, at, :]], 0))
            x = left(li[...], jnp.concatenate(cols, 1))
            for j in range(ZQ):
                z = p * ZQ + j
                br = x[:N, j * N:(j + 1) * N]
                bi = x[N:, j * N:(j + 1) * N]
                mr = maps[c, 0, z]
                mi = maps[c, 1, z]
                now = (mr * br + mi * bi, mr * bi - mi * br)
                for r in range(2):
                    sums[j][r] = now[r] if c == 0 else sums[j][r] + now[r]
        for j in range(ZQ):
            for r in range(2):
                v = sums[j][r].reshape(8, 2, B, N)
                for g in range(2):
                    part[p, g, :, r, j] = v[:, g]
        to_sibling(p).start()
        to_sibling(p).wait_recv()

        def rs_out(k):
            target = lax.rem(chip + k + 1, 8)
            rs_a[p, target] = rs_a[p, target] + part[p, core, target]
            rs_copy(p, target, chip).start()

        loop(7, rs_out)
        rs_b[p, chip] = rs_a[p, chip] + part[p, core, chip]
        ref = rs_b.at[p, pl.ds(0, 7)]
        pltpu.make_async_copy(ref, ref, rs_recv.at[p]).wait()
        total = rs_b[p, 0]
        for k in range(1, 8):
            total = total + rs_b[p, k]
        combined[:, pl.ds(p * ZQ, ZQ)] = total
        big[1, :, pl.ds(3 + p * ZQ, ZQ)] = total

    loop(Q, finish)

    near = [(a, b) for a in (-1, 0, 1) for b in (-1, 0, 1) if (a, b) != (0, 0)]
    source = {-1: (3, 3), 0: (3, 8), 1: (8, 3)}
    place = {-1: (11, 3), 0: (3, 8), 1: (0, 3)}
    copies = []
    for i, (dz, dx) in enumerate(near):
        a, n = source[dz]
        b, n = place[dz]
        copies.append(pltpu.make_async_remote_copy(
            src_ref=big.at[1, :, pl.ds(a, n)], dst_ref=big.at[1 - dx, :, pl.ds(b, n)],
            send_sem=halo_send.at[i], recv_sem=halo_recv.at[i],
            device_id=near_id(dz, dx), device_id_type=MESH))
        copies[-1].start()
    for copy in copies:
        copy.wait_recv()

    for z in range(14):
        rows = []
        for c in range(2):
            for blk in range(3):
                v = big[blk, c, z]
                if blk == 0:
                    v = jnp.where(me_c == 0, 0.0, v)
                if blk == 2:
                    v = jnp.where(me_c == G - 1, 0.0, v)
                if z < 3:
                    v = jnp.where(me_s == 0, 0.0, v)
                if z >= 11:
                    v = jnp.where(me_s == G - 1, 0.0, v)
                rows.append(v)
        hi, lo = split(jnp.concatenate(rows, 0))
        f0h[:, z * N:(z + 1) * N] = hi
        f0l[:, z * N:(z + 1) * N] = lo

    def inside(rows, first_x, z):
        x = me_c * B + first_x + lax.broadcasted_iota(jnp.int32, (rows, N), 0) // 32
        z = me_s * B + z
        return (x >= 0) & (x < N) & (z >= 0) & (z < N)

    def conv1(i):
        def planes(ref):
            return [ref[:, pl.ds(pl.multiple_of((2 * i + dz) * N, N), 2 * N)] for dz in range(3)]

        hi = planes(f0h)
        y = jnp.dot(w1[:, 0:432], jnp.concatenate(hi + planes(f0l) + hi, 0), preferred_element_type=F32)
        for j in range(2):
            p = [y[d * 384:(d + 1) * 384, j * N:(j + 1) * N] for d in range(3)]
            v = jnp.maximum(shifted_sum(*p), 0.0)
            v = jnp.where(inside(384, -2, 2 * i + j - 2), v, 0.0)
            hi_out, lo_out = split(v)
            at = pl.ds(pl.multiple_of((2 * i + j) * N, N), N)
            f1h[0:384, at] = hi_out
            f1l[0:384, at] = lo_out

    loop(6, conv1)

    def conv2(i):
        for g in range(2):
            parts = []
            for dz in range(3):
                at = pl.ds(pl.multiple_of((2 * i + dz) * N, N), 2 * N)
                hi = f1h[g * 160:g * 160 + 256, at]
                parts += [hi, f1l[g * 160:g * 160 + 256, at], hi]
            y = jnp.dot(w2[...], jnp.concatenate(parts, 0), preferred_element_type=F32)
            for j in range(2):
                p = [y[d * 160:(d + 1) * 160, j * N:(j + 1) * N] for d in range(3)]
                v = jnp.maximum(shifted_sum(*p), 0.0)
                v = jnp.where(inside(160, g * 5 - 1, 2 * i + j - 1), v, 0.0)
                hi, lo = split(v)
                at = pl.ds(pl.multiple_of((2 * i + j) * N, N), N)
                f2h[g * 160:(g + 1) * 160, at] = hi
                f2l[g * 160:(g + 1) * 160, at] = lo

    loop(5, conv2)

    def conv3(i):
        at = pl.ds(pl.multiple_of(2 * i * N, N), 2 * N)
        y = jnp.dot(w3[:, 0:320], f2h[:, at], preferred_element_type=F32)
        y = y[:144] + y[144:] + jnp.dot(w3[0:144, 0:320], f2l[:, at], preferred_element_type=F32)
        q3[2 * i] = y[:, :N]
        q3[2 * i + 1] = y[:, N:]

    loop(5, conv3)

    def last(z):
        p = []
        for dy in range(3):
            p.append(sum(q3[z + dz, dz * 48 + dy * 16:dz * 48 + dy * 16 + 16, :] for dz in range(3)))
        v = shifted_sum(*p)
        refined[0, z] = combined[0, z] + v[:B]
        refined[1, z] = combined[1, z] + v[B:]

    loop(B, last)

    for copy in copies:
        copy.wait_send()

    def drain(ref, sem):
        pltpu.make_async_copy(ref, ref, sem).wait()

    drain(gath.at[:, pl.ds(0, G - 1)], ag_send)
    drain(send1.at[:, :, pl.ds(0, Q * (CHUNK - ROWS))], a1_send)
    drain(send2.at[:, :, pl.ds(0, Q * (CHUNK - ROWS))], a2_send)
    drain(part.at[:, 0], sib_send)
    drain(rs_a.at[:, pl.ds(0, 7)], rs_send)


def body(estimate, coil_maps, measured, line_mask, w_first, w_middle, w_last):
    tabs = [jnp.asarray(t) for t in tables()]
    measured = measured.reshape(2, 2, N * B, N)
    operands = (estimate, coil_maps, measured, line_mask, w_first, w_middle, w_last, *tabs)
    vmem = pl.BlockSpec(memory_space=pltpu.VMEM)
    dma = pltpu.SemaphoreType.DMA
    block = jax.ShapeDtypeStruct((2, B, B, N), F32)
    return pl.pallas_call(
        kernel,
        out_shape=(block, block),
        in_specs=[pl.BlockSpec(memory_space=pl.ANY)] * len(operands),
        out_specs=(vmem, vmem),
        scratch_shapes=[pltpu.VMEM(a.shape, a.dtype) for a in (
            estimate, coil_maps, measured, line_mask, w_first, w_middle, w_last,
            tabs[0], tabs[1], tabs[2], tabs[3], tabs[4], tabs[5])] + [
            pltpu.VMEM((Q, G, 2, ZQ, B, N), F32),
            pltpu.VMEM((2, 2, N * B, N), F32),
            pltpu.VMEM((2, 2, N * B, N), F32),
            pltpu.VMEM((2, 2, N * B, N), F32),
            pltpu.VMEM((2, 2, N * B, N), F32),
            pltpu.VMEM((Q, 2, 8, 2, ZQ, B, N), F32),
            pltpu.VMEM((Q, 8, 2, ZQ, B, N), F32),
            pltpu.VMEM((Q, 8, 2, ZQ, B, N), F32),
            pltpu.VMEM((1152, 512), BF16),
            pltpu.VMEM((480, 2304), BF16),
            pltpu.VMEM((288, 384), BF16),
            pltpu.VMEM((3, 2, 14, B, N), F32),
            pltpu.VMEM((48, 14 * N), BF16), pltpu.VMEM((48, 14 * N), BF16),
            pltpu.VMEM((416, 12 * N), BF16), pltpu.VMEM((416, 12 * N), BF16),
            pltpu.VMEM((320, 10 * N), BF16), pltpu.VMEM((320, 10 * N), BF16),
            pltpu.VMEM((10, 144, N), F32),
            dma((13,)), dma, dma((Q, G)), dma, dma((2, Q)), dma, dma((2, Q)),
            dma, dma((Q,)), dma, dma((Q,)), dma((8,)), dma((8,)),
        ],
        compiler_params=pltpu.CompilerParams(
            collective_id=0, has_side_effects=True, vmem_limit_bytes=56 * 2**20),
    )(*operands)


def solution(mesh):
    in_specs = (
        P(None, "slab", "coil", None),
        P("coil", None, "slab", None, None),
        P("coil", None, None, "slab", None),
        P(),
        P(),
        P(),
        P(),
    )
    out_specs = (P(None, "slab", "coil", None), P(None, "slab", "coil", None))
    return jax.shard_map(body, mesh=mesh, in_specs=in_specs, out_specs=out_specs, check_vma=False)
```

time: 201 us -> 146 us (0.73)
  local copies, waits for them, and re-layouts: 35.1 us -> 4.69 us
  Pallas kernels: 153 us -> 140 us
  matrix products: 9.55 us -> 0 us
    pallas_call x2 -> x1, Pallas kernels: 153 us -> 140 us  [body(): pl.pallas_call(kernel, out_shape=(block, block), in_specs=[pl.BlockSpec(m...]
    dot_general x3 -> x0, matrix products: 9.55 us -> none  [the longest x1 6.1 us: conv_weights(): jnp.einsum('zxyoc,pxq->ypozqc', w_middle.reshape(3, 3, 3, 32, 32), select...]
    reshape x3 -> x0, local copies, waits for them, and re-layouts: 8.97 us -> none  [the longest x1 4.17 us: conv_weights(): w2 = pieces(w2.reshape(480, 3, 256), 2).reshape(480, 2304)]
    transpose x3 -> x0, local copies, waits for them, and re-layouts: 6.66 us -> none  [the longest x1 2.91 us: conv_weights(): jnp.einsum('zxyoc,pxq->ypozqc', w_middle.reshape(3, 3, 3, 32, 32), select...]
    convert_element_type x3 -> x0, local copies, waits for them, and re-layouts: 6.63 us -> none  [pieces(): return jnp.stack([hi, hi, w - hi], axis).astype(BF16)]
    another operation x3 -> x0, local copies, waits for them, and re-layouts: 4.44 us -> none  [pieces(): return jnp.stack([hi, hi, w - hi], axis).astype(BF16)]
    unnamed x28 -> x3, local copies, waits for them, and re-layouts: 8.45 us -> 4.69 us
where the time goes in v2:
time: 146 us
  Pallas kernels  140 us (96%)
  local copies, waits for them, and re-layouts  4.69 us (3%)
    pallas_call x1, Pallas kernels, body(): pl.pallas_call(kernel, out_shape=(block, block), in_specs=[pl.BlockSpec(m...  140 us
    unnamed x3, local copies, waits for them, and re-layouts  4.69 us

profile of v2, /device:TPU:1, one launch (start us, length us, event | category | flops | bytes accessed | tf_op | source)
XLA Modules:
  0.0 145.8 jit_solution(5343880279977061754)
XLA Ops:
  0.6 1.7 %copy.15.wf_in = f32[27,32,2]{2,1,0:T(8,128)} copy(f32[27,32,2]{1,2,0:T(2,128)} %param.17) | data formatting | bytes 13824 | tf_op args[4]
  2.4 140.5 %shard_map.140 = (f32[2,8,8,128]{3,2,1,0:T(8,128)}, f32[2,8,8,128]{3,2,1,0:T(8,128)}) custom-call(f32[2,8,8,128]{3,2,1,0:T(8,128)} %est_in.1, f32[2,2,8,128,128]{4,3,2,1,0:T(8,128)} %maps_in.1, f32[2,2,1024,128]{3,2,1,0:T(8,128)} %bitcast.1, s32[128,128]{1,0:T(8,128)} %mask_in.1, f32[27,32,2]{2,1,0:T(8,128)} %copy.15.wf_in, f32[27,32,32]{2,1,0:T(8,128)} %wm_in.1, ...), custom_call_target="tpu_custom_call" | custom-call | tf_op jit(solution)/shard_map/pallas_call | solution.py:446
  142.8 1.5 %copy.18 = f32[2,8,8,128]{3,2,1,0:T(8,128)} copy(f32[2,8,8,128]{3,2,1,0:T(8,128)} %get-tuple-element.4) | data formatting | bytes 131072
  144.3 1.5 %copy.19 = f32[2,8,8,128]{3,2,1,0:T(8,128)} copy(f32[2,8,8,128]{3,2,1,0:T(8,128)} %get-tuple-element.5) | data formatting | bytes 131072

commit v3 on v2

--- a/solution.py
+++ b/solution.py
@@ -83,24 +83,23 @@
         base = jnp.zeros((32, 512), F32)
         for dz in range(3):
             for dx in range(3):
-                taps = wf[dz * 9 + dx * 3 + dy]
+                taps = jnp.transpose(jnp.concatenate([wf[dz * 9 + dx * 3 + dy], jnp.zeros((6, 32), F32)], 0))
                 for c in range(2):
                     base = jnp.where(lane == dz * 48 + c * 24 + dx + 5, taps[:, c:c + 1], base)
         hi = base.astype(BF16).astype(F32)
         full = hi + pltpu.roll(hi, 144, 1) + pltpu.roll(base - hi, 288, 1)
         for xo in range(12):
-            r = (dy * 12 + xo) * 32
+            r = xo // 4 * 384 + dy * 128 + xo % 4 * 32
             w1[r:r + 32, :] = (pltpu.roll(full, xo, 1) if xo else full).astype(BF16)
     for dz in range(3):
         for dy in range(3):
             base = jnp.concatenate(
-                [wm[dz * 9 + dx * 3 + dy] for dx in range(3)] + [jnp.zeros((32, 160), F32)], 1)
-            for xo in range(5):
-                hi, lo = split(pltpu.roll(base, 32 * xo, 1) if xo else base)
-                r = (dy * 5 + xo) * 32
-                w2[r:r + 32, dz * 768:dz * 768 + 256] = hi
-                w2[r:r + 32, dz * 768 + 256:dz * 768 + 512] = hi
-                w2[r:r + 32, dz * 768 + 512:dz * 768 + 768] = lo
+                [wm[dz * 9 + dx * 3 + dy] for dx in range(3)] + [jnp.zeros((32, 32), F32)], 1)
+            for xo in range(2):
+                hi, lo = split(pltpu.roll(base, 32, 1) if xo else base)
+                r = (dy * 2 + xo) * 32
+                for part, value in enumerate((hi, hi, lo)):
+                    w2[r:r + 32, part * 384 + dz * 128:part * 384 + dz * 128 + 128] = value
     for dz in range(3):
         for dy in range(3):
             base = jnp.concatenate(
@@ -157,8 +156,7 @@
             src_ref=src, dst_ref=gath.at[q, slot], send_sem=ag_send, recv_sem=ag_recv.at[q, slot],
             device_id={"coil": target}, device_id_type=MESH)
 
-    loads[0].wait()
-    for q in range(Q):
+    def gather_out(q):
         mine = est.at[:, pl.ds(q * ZQ, ZQ)]
 
         def ag_out(k):
@@ -214,8 +212,13 @@
                 send1[c, r, pl.ds(q * CHUNK + j, N, stride=ZQ), :] = y[r * N:(r + 1) * N, j * N:(j + 1) * N]
         exchange_out(send1, recv1, c, q, a1_send, a1_recv)
 
-    forward(0)
+    loads[0].wait()
+    gather_out(0)
     for q in range(Q):
+        forward(q)
+        if q + 1 < Q:
+            gather_out(q + 1)
+
         def ag_last(k):
             slot = 2 * lax.rem(chip + 8 - k, 8) + 1 - core
             ag_copy(gath.at[q, slot], q, slot, sibling).wait_recv()
@@ -225,15 +228,11 @@
             loads[1].wait()
             loads[2].wait()
         slab_chunk(0, q)
-        if q + 1 < Q:
-            forward(q + 1)
     loop(Q, lambda q: slab_chunk(1, q))
 
     for load in loads[3:]:
         load.wait()
     build_weights(wf, wm, wl, w1, w2, w3)
-    f1h[384:, :] = jnp.zeros((32, 12 * N), BF16)
-    f1l[384:, :] = jnp.zeros((32, 12 * N), BF16)
 
     def pencils(c):
         loop(Q, lambda q: exchange_in(recv1, c, q, a1_recv))
@@ -286,132 +285,151 @@
             src_ref=rs_a.at[p, target], dst_ref=rs_b.at[p, slot], send_sem=rs_send, recv_sem=rs_recv.at[p],
             device_id={"coil": 2 * target + core}, device_id_type=MESH)
 
-    def finish(p):
-        exchange_in(recv2, 0, p, a2_recv)
-        exchange_in(recv2, 1, p, a2_recv)
-        sums = [[None, None] for j in range(ZQ)]
-        for c in range(2):
-            cols = []
-            for j in range(ZQ):
-                at = pl.ds(p * CHUNK + j, N, stride=ZQ)
-                cols.append(jnp.concatenate([recv2[c, 0, at, :], recv2[c, 1, at, :]], 0))
-            x = left(li[...], jnp.concatenate(cols, 1))
-            for j in range(ZQ):
-                z = p * ZQ + j
-                br = x[:N, j * N:(j + 1) * N]
-                bi = x[N:, j * N:(j + 1) * N]
-                mr = maps[c, 0, z]
-                mi = maps[c, 1, z]
-                now = (mr * br + mi * bi, mr * bi - mi * br)
-                for r in range(2):
-                    sums[j][r] = now[r] if c == 0 else sums[j][r] + now[r]
+    def coil_back(c, p):
+        exchange_in(recv2, c, p, a2_recv)
+        cols = []
         for j in range(ZQ):
-            for r in range(2):
-                v = sums[j][r].reshape(8, 2, B, N)
+            at = pl.ds(p * CHUNK + j, N, stride=ZQ)
+            cols.append(jnp.concatenate([recv2[c, 0, at, :], recv2[c, 1, at, :]], 0))
+        x = left(li[...], jnp.concatenate(cols, 1))
+        for j in range(ZQ):
+            z = p * ZQ + j
+            br = x[:N, j * N:(j + 1) * N]
+            bi = x[N:, j * N:(j + 1) * N]
+            mr = maps[c, 0, z]
+            mi = maps[c, 1, z]
+            for r, v in enumerate((mr * br + mi * bi, mr * bi - mi * br)):
+                v = v.reshape(8, 2, B, N)
                 for g in range(2):
-                    part[p, g, :, r, j] = v[:, g]
-        to_sibling(p).start()
-        to_sibling(p).wait_recv()
-
+                    part[p, g, :, r, j] = v[:, g] if c == 0 else part[p, g, :, r, j] + v[:, g]
+
+    near = [(a, b) for a in (-1, 0, 1) for b in (-1, 0, 1) if (a, b) != (0, 0)]
+
+    def halo(dz, dx, p=0):
+        a, b, n = {-1: (3, 11, 3), 0: (3 + p * ZQ, 3 + p * ZQ, ZQ), 1: (8, 0, 3)}[dz]
+        i = 3 * (dz > 0) + 6 * (dz == 0) + (dx + 1 if dz else p * 2 + (dx + 1) // 2)
+        return pltpu.make_async_remote_copy(
+            src_ref=big.at[1, :, pl.ds(a, n)], dst_ref=big.at[1 - dx, :, pl.ds(b, n)],
+            send_sem=halo_send.at[i], recv_sem=halo_recv.at[i],
+            device_id=near_id(dz, dx), device_id_type=MESH)
+
+    def spread(p):
         def rs_out(k):
             target = lax.rem(chip + k + 1, 8)
             rs_a[p, target] = rs_a[p, target] + part[p, core, target]
             rs_copy(p, target, chip).start()
 
+        to_sibling(p).wait_recv()
         loop(7, rs_out)
         rs_b[p, chip] = rs_a[p, chip] + part[p, core, chip]
+
+    def total(p):
         ref = rs_b.at[p, pl.ds(0, 7)]
         pltpu.make_async_copy(ref, ref, rs_recv.at[p]).wait()
-        total = rs_b[p, 0]
+        value = rs_b[p, 0]
         for k in range(1, 8):
-            total = total + rs_b[p, k]
-        combined[:, pl.ds(p * ZQ, ZQ)] = total
-        big[1, :, pl.ds(3 + p * ZQ, ZQ)] = total
-
-    loop(Q, finish)
-
-    near = [(a, b) for a in (-1, 0, 1) for b in (-1, 0, 1) if (a, b) != (0, 0)]
-    source = {-1: (3, 3), 0: (3, 8), 1: (8, 3)}
-    place = {-1: (11, 3), 0: (3, 8), 1: (0, 3)}
-    copies = []
-    for i, (dz, dx) in enumerate(near):
-        a, n = source[dz]
-        b, n = place[dz]
-        copies.append(pltpu.make_async_remote_copy(
-            src_ref=big.at[1, :, pl.ds(a, n)], dst_ref=big.at[1 - dx, :, pl.ds(b, n)],
-            send_sem=halo_send.at[i], recv_sem=halo_recv.at[i],
-            device_id=near_id(dz, dx), device_id_type=MESH))
-        copies[-1].start()
-    for copy in copies:
-        copy.wait_recv()
-
-    for z in range(14):
+            value = value + rs_b[p, k]
+        big[1, :, 3 + p * ZQ:3 + (p + 1) * ZQ] = value
+        halo(0, -1, p).start()
+        halo(0, 1, p).start()
+        if p in (1, 3):
+            for dx in (0, -1, 1):
+                halo(p - 2, dx).start()
+        combined[:, p * ZQ:(p + 1) * ZQ] = value
+
+    loop(Q, lambda p: coil_back(0, p))
+    for p in range(Q):
+        coil_back(1, p)
+        to_sibling(p).start()
+        if p:
+            total(p - 1)
+        spread(p)
+    total(Q - 1)
+
+    low_c, high_c, low_s, high_s = me_c == 0, me_c == G - 1, me_s == 0, me_s == G - 1
+
+    def guard(v, *outside):
+        for out, here in outside:
+            if here:
+                v = jnp.where(out, 0.0, v)
+        return v
+
+    def layer0(z):
         rows = []
         for c in range(2):
             for blk in range(3):
-                v = big[blk, c, z]
-                if blk == 0:
-                    v = jnp.where(me_c == 0, 0.0, v)
-                if blk == 2:
-                    v = jnp.where(me_c == G - 1, 0.0, v)
-                if z < 3:
-                    v = jnp.where(me_s == 0, 0.0, v)
-                if z >= 11:
-                    v = jnp.where(me_s == G - 1, 0.0, v)
-                rows.append(v)
-        hi, lo = split(jnp.concatenate(rows, 0))
-        f0h[:, z * N:(z + 1) * N] = hi
-        f0l[:, z * N:(z + 1) * N] = lo
-
-    def inside(rows, first_x, z):
-        x = me_c * B + first_x + lax.broadcasted_iota(jnp.int32, (rows, N), 0) // 32
-        z = me_s * B + z
-        return (x >= 0) & (x < N) & (z >= 0) & (z < N)
+                rows.append(guard(
+                    big[blk, c, z], (low_c, blk == 0), (high_c, blk == 2), (low_s, z < 3), (high_s, z >= 11)))
+        f0h[:, z * N:(z + 1) * N], f0l[:, z * N:(z + 1) * N] = split(jnp.concatenate(rows, 0))
+
+    def window(hi, lo, i, rows):
+        h = [hi[rows, (2 * i + dz) * N:(2 * i + dz + 2) * N] for dz in range(3)]
+        l = [lo[rows, (2 * i + dz) * N:(2 * i + dz + 2) * N] for dz in range(3)]
+        return jnp.concatenate(h + l + h, 0)
 
     def conv1(i):
-        def planes(ref):
-            return [ref[:, pl.ds(pl.multiple_of((2 * i + dz) * N, N), 2 * N)] for dz in range(3)]
-
-        hi = planes(f0h)
-        y = jnp.dot(w1[:, 0:432], jnp.concatenate(hi + planes(f0l) + hi, 0), preferred_element_type=F32)
-        for j in range(2):
-            p = [y[d * 384:(d + 1) * 384, j * N:(j + 1) * N] for d in range(3)]
-            v = jnp.maximum(shifted_sum(*p), 0.0)
-            v = jnp.where(inside(384, -2, 2 * i + j - 2), v, 0.0)
-            hi_out, lo_out = split(v)
-            at = pl.ds(pl.multiple_of((2 * i + j) * N, N), N)
-            f1h[0:384, at] = hi_out
-            f1l[0:384, at] = lo_out
-
-    loop(6, conv1)
+        data = window(f0h, f0l, i, slice(0, 48))
+        for g in range(3):
+            y = jnp.dot(w1[g * 384:(g + 1) * 384, 0:432], data, preferred_element_type=F32)
+            for j in range(2):
+                z = 2 * i + j
+                v = jnp.maximum(shifted_sum(*[y[d * 128:(d + 1) * 128, j * N:(j + 1) * N] for d in range(3)]), 0.0)
+                v = guard(v, (low_s, z < 2), (high_s, z >= 10))
+                v = jnp.concatenate([
+                    guard(v[:64], (low_c, g == 0)), guard(v[64:], (high_c, g == 2))], 0)
+                at = (slice(g * 128, (g + 1) * 128), slice(z * N, (z + 1) * N))
+                f1h[at], f1l[at] = split(v)
 
     def conv2(i):
-        for g in range(2):
-            parts = []
-            for dz in range(3):
-                at = pl.ds(pl.multiple_of((2 * i + dz) * N, N), 2 * N)
-                hi = f1h[g * 160:g * 160 + 256, at]
-                parts += [hi, f1l[g * 160:g * 160 + 256, at], hi]
-            y = jnp.dot(w2[...], jnp.concatenate(parts, 0), preferred_element_type=F32)
+        for g in range(5):
+            data = window(f1h, f1l, i, slice(g * 64, g * 64 + 128))
+            y = jnp.dot(w2[...], data, preferred_element_type=F32)
             for j in range(2):
-                p = [y[d * 160:(d + 1) * 160, j * N:(j + 1) * N] for d in range(3)]
-                v = jnp.maximum(shifted_sum(*p), 0.0)
-                v = jnp.where(inside(160, g * 5 - 1, 2 * i + j - 1), v, 0.0)
-                hi, lo = split(v)
-                at = pl.ds(pl.multiple_of((2 * i + j) * N, N), N)
-                f2h[g * 160:(g + 1) * 160, at] = hi
-                f2l[g * 160:(g + 1) * 160, at] = lo
-
-    loop(5, conv2)
+                z = 2 * i + j
+                v = jnp.maximum(shifted_sum(*[y[d * 64:(d + 1) * 64, j * N:(j + 1) * N] for d in range(3)]), 0.0)
+                v = guard(v, (low_s, z < 1), (high_s, z >= 9))
+                v = jnp.concatenate([
+                    guard(v[:32], (low_c, g == 0)), guard(v[32:], (high_c, g == 4))], 0)
+                at = (slice(g * 64, (g + 1) * 64), slice(z * N, (z + 1) * N))
+                f2h[at], f2l[at] = split(v)
 
     def conv3(i):
-        at = pl.ds(pl.multiple_of(2 * i * N, N), 2 * N)
+        at = slice(2 * i * N, (2 * i + 2) * N)
         y = jnp.dot(w3[:, 0:320], f2h[:, at], preferred_element_type=F32)
         y = y[:144] + y[144:] + jnp.dot(w3[0:144, 0:320], f2l[:, at], preferred_element_type=F32)
         q3[2 * i] = y[:, :N]
         q3[2 * i + 1] = y[:, N:]
 
-    loop(5, conv3)
+    for p in range(3):
+        halo(0, -1, p).wait_recv()
+        halo(0, 1, p).wait_recv()
+    for z in range(3, 9):
+        layer0(z)
+    conv1(2)
+    for dx in (-1, 0, 1):
+        halo(-1, dx).wait_recv()
+    for z in range(11, 14):
+        layer0(z)
+    halo(0, -1, 3).wait_recv()
+    halo(0, 1, 3).wait_recv()
+    layer0(9)
+    layer0(10)
+    for i in (3, 4, 5):
+        conv1(i)
+    for i in (2, 3, 4):
+        conv2(i)
+    for i in (2, 3, 4):
+        conv3(i)
+    for dx in (-1, 0, 1):
+        halo(1, dx).wait_recv()
+    for z in range(3):
+        layer0(z)
+    conv1(0)
+    conv1(1)
+    conv2(0)
+    conv2(1)
+    conv3(0)
+    conv3(1)
 
     def last(z):
         p = []
@@ -421,10 +439,12 @@
         refined[0, z] = combined[0, z] + v[:B]
         refined[1, z] = combined[1, z] + v[B:]
 
-    loop(B, last)
-
-    for copy in copies:
-        copy.wait_send()
+    for z in range(B):
+        last(z)
+
+    for dz, dx in near:
+        for p in range(1 if dz else Q):
+            halo(dz, dx, p).wait_send()
 
     def drain(ref, sem):
         pltpu.make_async_copy(ref, ref, sem).wait()
@@ -436,14 +456,23 @@
     drain(rs_a.at[:, pl.ds(0, 7)], rs_send)
 
 
+def hand_over(a_in, b_in, a_out, b_out, sem):
+    copies = [pltpu.make_async_copy(a_in, a_out, sem.at[0]), pltpu.make_async_copy(b_in, b_out, sem.at[1])]
+    for copy in copies:
+        copy.start()
+    for copy in copies:
+        copy.wait()
+
+
 def body(estimate, coil_maps, measured, line_mask, w_first, w_middle, w_last):
     tabs = [jnp.asarray(t) for t in tables()]
     measured = measured.reshape(2, 2, N * B, N)
+    w_first = jnp.transpose(w_first, (0, 2, 1))
     operands = (estimate, coil_maps, measured, line_mask, w_first, w_middle, w_last, *tabs)
     vmem = pl.BlockSpec(memory_space=pltpu.VMEM)
     dma = pltpu.SemaphoreType.DMA
     block = jax.ShapeDtypeStruct((2, B, B, N), F32)
-    return pl.pallas_call(
+    results = pl.pallas_call(
         kernel,
         out_shape=(block, block),
         in_specs=[pl.BlockSpec(memory_space=pl.ANY)] * len(operands),
@@ -460,19 +489,27 @@
             pltpu.VMEM((Q, 8, 2, ZQ, B, N), F32),
             pltpu.VMEM((Q, 8, 2, ZQ, B, N), F32),
             pltpu.VMEM((1152, 512), BF16),
-            pltpu.VMEM((480, 2304), BF16),
+            pltpu.VMEM((192, 1152), BF16),
             pltpu.VMEM((288, 384), BF16),
             pltpu.VMEM((3, 2, 14, B, N), F32),
             pltpu.VMEM((48, 14 * N), BF16), pltpu.VMEM((48, 14 * N), BF16),
-            pltpu.VMEM((416, 12 * N), BF16), pltpu.VMEM((416, 12 * N), BF16),
+            pltpu.VMEM((384, 12 * N), BF16), pltpu.VMEM((384, 12 * N), BF16),
             pltpu.VMEM((320, 10 * N), BF16), pltpu.VMEM((320, 10 * N), BF16),
             pltpu.VMEM((10, 144, N), F32),
             dma((13,)), dma, dma((Q, G)), dma, dma((2, Q)), dma, dma((2, Q)),
-            dma, dma((Q,)), dma, dma((Q,)), dma((8,)), dma((8,)),
+            dma, dma((Q,)), dma, dma((Q,)), dma((14,)), dma((14,)),
         ],
         compiler_params=pltpu.CompilerParams(
             collective_id=0, has_side_effects=True, vmem_limit_bytes=56 * 2**20),
     )(*operands)
+    anywhere = pl.BlockSpec(memory_space=pl.ANY)
+    return pl.pallas_call(
+        hand_over,
+        out_shape=(block, block),
+        in_specs=[anywhere] * 2,
+        out_specs=(anywhere, anywhere),
+        scratch_shapes=[dma((2,))],
+    )(*results)
 
 
 def solution(mesh):

time: 146 us -> 133 us (0.911)
  Pallas kernels: 140 us -> 133 us
  local copies, waits for them, and re-layouts: 4.69 us -> 0 us
    pallas_call x1, Pallas kernels: 140 us -> 128 us  [body(): pl.pallas_call(kernel, out_shape=(block, block), in_specs=[pl.BlockSpec(m...]
    pallas_call x0 -> x1, Pallas kernels: none -> 5.09 us  [body(): pl.pallas_call(hand_over, out_shape=(block, block), in_specs=[anywhere] *...]
    unnamed x3 -> x0, local copies, waits for them, and re-layouts: 4.69 us -> none
where the time goes in v3:
time: 133 us
  Pallas kernels  133 us (100%)
    pallas_call x1, Pallas kernels, body(): pl.pallas_call(kernel, out_shape=(block, block), in_specs=[pl.BlockSpec(m...  128 us
    pallas_call x1, Pallas kernels, body(): pl.pallas_call(hand_over, out_shape=(block, block), in_specs=[anywhere] *...  5.09 us

profile of v3, /device:TPU:1, one launch (start us, length us, event | category | flops | bytes accessed | tf_op | source)
XLA Modules:
  0.0 133.4 jit_solution(7141798059505653629)
XLA Ops:
  0.6 127.7 %shard_map.140 = (f32[2,8,8,128]{3,2,1,0:T(8,128)}, f32[2,8,8,128]{3,2,1,0:T(8,128)}) custom-call(f32[2,8,8,128]{3,2,1,0:T(8,128)} %est_in.1, f32[2,2,8,128,128]{4,3,2,1,0:T(8,128)} %maps_in.1, f32[2,2,1024,128]{3,2,1,0:T(8,128)} %bitcast.2, s32[128,128]{1,0:T(8,128)} %mask_in.1, f32[27,2,32]{2,1,0:T(2,128)} %bitcast.3, f32[27,32,32]{2,1,0:T(8,128)} %wm_in.1, ...), custom_call_target="tpu_custom_call" | custom-call | tf_op jit(solution)/shard_map/pallas_call | solution.py:475
  128.3 5.1 %shard_map.141 = (f32[2,8,8,128]{3,2,1,0:T(8,128)}, f32[2,8,8,128]{3,2,1,0:T(8,128)}) custom-call(f32[2,8,8,128]{3,2,1,0:T(8,128)} %get-tuple-element.4.a_in, f32[2,8,8,128]{3,2,1,0:T(8,128)} %get-tuple-element.5.b_in), custom_call_target="tpu_custom_call" | custom-call | tf_op jit(solution)/shard_map/pallas_call | solution.py:506

commit v4 on v3

v4 whole, which is shorter than its diff:
```python
import math

import jax
import jax.numpy as jnp
import ml_dtypes
import numpy as np
from jax import lax
from jax.experimental import pallas as pl
from jax.experimental.pallas import tpu as pltpu
from jax.sharding import PartitionSpec as P

MESH = pl.DeviceIdType.MESH
F32 = jnp.float32
BF16 = jnp.bfloat16
N = 128
B = 8
G = 16
ROWS = B
CHUNK = G * ROWS


def tables():
    k = np.arange(N)
    angle = 2.0 * math.pi * (np.outer(k, k) % N) / N
    c, s = np.cos(angle) / math.sqrt(N), np.sin(angle) / math.sqrt(N)
    fwd = np.block([[c, s], [-s, c]])
    inv = np.block([[c, -s], [s, c]])

    def pieces(m):
        hi = m.astype(np.float32).astype(ml_dtypes.bfloat16)
        lo = (m - hi.astype(np.float64)).astype(np.float32).astype(ml_dtypes.bfloat16)
        return [hi, hi, lo]

    order = np.arange(N).reshape(G, B).T.reshape(-1)
    order = np.concatenate([order, order + N])
    return [
        np.concatenate(pieces(fwd), 1),
        np.concatenate(pieces(inv), 1),
        np.concatenate(pieces(inv), 0),
        np.concatenate(pieces(fwd), 0),
        np.concatenate(pieces(fwd[:, order]), 1),
        np.concatenate(pieces(inv[order]), 1),
    ]


def split(x):
    hi = x.astype(BF16)
    lo = (x - hi.astype(F32)).astype(BF16)
    return hi, lo


def left(table, x):
    hi, lo = split(x)
    return jnp.dot(table, jnp.concatenate([hi, lo, hi], 0), preferred_element_type=F32)


def right(x, table):
    hi, lo = split(x)
    return jnp.dot(jnp.concatenate([hi, lo, hi], 1), table, preferred_element_type=F32)


def loop(count, fn):
    def step(i, carry):
        fn(i)
        return carry

    lax.fori_loop(0, count, step, 0)


def shifted_sum(p0, p1, p2):
    lane = lax.broadcasted_iota(jnp.int32, p0.shape, 1)
    down = jnp.where(lane == 0, 0.0, pltpu.roll(p0, 1, 1))
    up = jnp.where(lane == N - 1, 0.0, pltpu.roll(p2, N - 1, 1))
    return p1 + down + up


def build_weights(wf, wm, wl, w1, w2, w3, depth):
    lane = lax.broadcasted_iota(jnp.int32, (32, 512), 1)
    for dy in range(3):
        base = jnp.zeros((32, 512), F32)
        for dz in range(3):
            for dx in range(3):
                taps = jnp.transpose(jnp.concatenate([wf[depth(dz) * 9 + dx * 3 + dy], jnp.zeros((6, 32), F32)], 0))
                for c in range(2):
                    base = jnp.where(lane == dz * 48 + c * 24 + dx + 5, taps[:, c:c + 1], base)
        hi = base.astype(BF16).astype(F32)
        full = hi + pltpu.roll(hi, 144, 1) + pltpu.roll(base - hi, 288, 1)
        for xo in range(12):
            r = xo // 4 * 384 + dy * 128 + xo % 4 * 32
            w1[r:r + 32, :] = (pltpu.roll(full, xo, 1) if xo else full).astype(BF16)
    for dz in range(3):
        for dy in range(3):
            base = jnp.concatenate(
                [wm[depth(dz) * 9 + dx * 3 + dy] for dx in range(3)] + [jnp.zeros((32, 32), F32)], 1)
            for xo in range(2):
                hi, lo = split(pltpu.roll(base, 32, 1) if xo else base)
                r = (dy * 2 + xo) * 32
                for part, value in enumerate((hi, hi, lo)):
                    w2[r:r + 32, part * 384 + dz * 128:part * 384 + dz * 128 + 128] = value
    for dz in range(3):
        for dy in range(3):
            base = jnp.concatenate(
                [wl[depth(dz) * 9 + dx * 3 + dy] for dx in range(3)] + [jnp.zeros((2, 416), F32)], 1)
            both = jnp.concatenate([jnp.broadcast_to(base[o:o + 1], (8, 512)) for o in range(2)], 0)
            row = lax.broadcasted_iota(jnp.int32, (16, 512), 0) % 8
            moved = both
            for xo in range(1, 8):
                moved = jnp.where(row == xo, pltpu.roll(both, 32 * xo, 1), moved)
            hi, lo = split(moved[:, :384])
            r = dz * 48 + dy * 16
            w3[r:r + 16, :] = hi
            w3[144 + r:160 + r, :] = lo


def kernel(
    est_in, maps_in, meas_in, mask_in, wf_in, wm_in, wl_in, t0, t1, t2, t3, t4, t5,
    combined, refined,
    est, maps, meas, mask, wf, wm, wl, lf, li, rf, ri_, lzf, lzi,
    gath, send1, recv1, send2, recv2, part, sums,
    w1, w2, w3, big, f0h, f0l, f1h, f1l, f2h, f2l, q3,
    load_sem, ag_send, ag_recv, a1_send, a1_recv, a2_send, a2_recv,
    rs_send, rs_recv, halo_send, halo_recv,
):
    me_c = lax.axis_index("coil")
    me_s = lax.axis_index("slab")
    odd = lax.rem(me_s, 2)
    sign = 1 - 2 * odd

    def plane(t):
        return (B - 1) * odd + sign * t

    barrier = pltpu.get_barrier_semaphore()

    def near_id(dz, dx):
        return {"coil": lax.rem(me_c + dx + G, G), "slab": lax.rem(me_s + sign * dz + G, G)}

    def greet(target):
        pl.semaphore_signal(barrier, inc=1, device_id=target, device_id_type=MESH)

    def greet_lines(k):
        greet({"coil": lax.rem(me_c + k + 1, G)})
        greet({"slab": lax.rem(me_s + k + 1, G)})

    loop(G - 1, greet_lines)
    for dz in (-1, 1):
        for dx in (-1, 1):
            greet(near_id(dz, dx))

    pairs = [(est_in, est), (t0, lf), (maps_in, maps), (wf_in, wf), (wm_in, wm), (wl_in, wl), (t2, rf), (t4, lzf),
             (meas_in, meas), (mask_in, mask), (t5, lzi), (t3, ri_), (t1, li)]
    loads = [pltpu.make_async_copy(a, b, load_sem.at[i]) for i, (a, b) in enumerate(pairs)]
    for load in loads:
        load.start()
    pl.semaphore_wait(barrier, 2 * (G - 1) + 4)

    def gather_out(q):
        def out(k):
            pltpu.make_async_remote_copy(
                src_ref=est.at[:, q], dst_ref=gath.at[q, me_c], send_sem=ag_send, recv_sem=ag_recv.at[q],
                device_id={"coil": lax.rem(me_c + k + 1, G)}, device_id_type=MESH).start()

        loop(G - 1, out)
        gath[q, me_c] = est[:, q]

    def gather_in(q):
        ref = gath.at[q, pl.ds(0, G - 1)]
        pltpu.make_async_copy(ref, ref, ag_recv.at[q]).wait()

    def exchange(buf, dst, c, q, peer, send_sem, recv_sem, turned):
        at = q + lax.rem(peer, 2) * (B - 1 - 2 * q) if turned else q
        return pltpu.make_async_remote_copy(
            src_ref=buf.at[c, :, pl.ds(pl.multiple_of(at * CHUNK + peer * ROWS, ROWS), ROWS), :],
            dst_ref=dst.at[c, :, pl.ds(pl.multiple_of(at * CHUNK + me_s * ROWS, ROWS), ROWS), :],
            send_sem=send_sem, recv_sem=recv_sem.at[c, q],
            device_id={"slab": peer}, device_id_type=MESH)

    def exchange_out(buf, dst, c, q, send_sem, recv_sem, turned=False):
        def out(k):
            exchange(buf, dst, c, q, lax.rem(me_s + k + 1, G), send_sem, recv_sem, turned).start()

        loop(G - 1, out)
        at = plane(q) if turned else q
        own = pl.ds(pl.multiple_of(at * CHUNK + me_s * ROWS, ROWS), ROWS)
        for r in range(2):
            dst[c, r, own, :] = buf[c, r, own, :]

    def all_of(buf, c, q):
        return buf.at[c, :, pl.ds(pl.multiple_of(q * CHUNK, CHUNK), CHUNK - ROWS), :]

    def exchange_in(dst, c, q, recv_sem):
        ref = all_of(dst, c, q)
        pltpu.make_async_copy(ref, ref, recv_sem.at[c, q]).wait()

    def slab_plane(c, q):
        ir = gath[q, :, 0].reshape(N, N)
        ii = gath[q, :, 1].reshape(N, N)
        mr = maps[c, 0, q]
        mi = maps[c, 1, q]
        y = left(lf[...], jnp.concatenate([mr * ir - mi * ii, mr * ii + mi * ir], 0))
        for r in range(2):
            send1[c, r, pl.ds(pl.multiple_of(q * CHUNK, CHUNK), CHUNK), :] = y[r * N:(r + 1) * N]
        exchange_out(send1, recv1, c, q, a1_send, a1_recv)

    loads[0].wait()
    gather_out(0)
    gather_out(1)
    loads[1].wait()
    loads[2].wait()
    for q in range(B):
        gather_in(q)
        if q + 2 < B:
            gather_out(q + 2)
        slab_plane(0, q)
    loop(B, lambda q: slab_plane(1, q))

    for load in loads[3:]:
        load.wait()
    build_weights(wf, wm, wl, w1, w2, w3, lambda dz: 2 * odd + sign * dz)

    def pencils(c):
        loop(B, lambda q: exchange_in(recv1, c, q, a1_recv))

        def pair(kp):
            rows = []
            for j in range(2):
                rows.append(jnp.concatenate(
                    [recv1[c, r, pl.ds(2 * kp + j, N, stride=ROWS), :] for r in range(2)], 1))
            y = right(jnp.concatenate(rows, 0), rf[...])
            x = jnp.concatenate([
                jnp.concatenate([y[:N, :N], y[N:, :N]], 1),
                jnp.concatenate([y[:N, N:], y[N:, N:]], 1)], 0)
            x = left(lzf[...], x)
            w = jnp.where(mask[...] == 1, 0.5, 0.0)
            halves = []
            for r in range(2):
                pieces = []
                for j in range(2):
                    k = x[r * N:(r + 1) * N, j * N:(j + 1) * N]
                    m = meas[c, r, pl.ds(2 * kp + j, N, stride=B), :]
                    pieces.append(k - w * (k - m))
                halves.append(jnp.concatenate(pieces, 1))
            x = left(lzi[...], jnp.concatenate(halves, 0))
            y = jnp.concatenate([
                jnp.concatenate([x[:N, :N], x[N:, :N]], 1),
                jnp.concatenate([x[:N, N:], x[N:, N:]], 1)], 0)
            y = right(y, ri_[...])
            for j in range(2):
                for r in range(2):
                    send2[c, r, pl.ds(2 * kp + j, N, stride=ROWS), :] = y[j * N:(j + 1) * N, r * N:(r + 1) * N]

        loop(4, pair)
        loop(B, lambda p: exchange_out(send2, recv2, c, p, a2_send, a2_recv, True))

    loop(2, pencils)

    def coil_back(c, p):
        exchange_in(recv2, c, p, a2_recv)
        z = plane(p)
        at = pl.ds(pl.multiple_of(z * CHUNK, CHUNK), CHUNK)
        x = left(li[...], jnp.concatenate([recv2[c, 0, at, :], recv2[c, 1, at, :]], 0))
        br = x[:N]
        bi = x[N:]
        mr = maps[c, 0, z]
        mi = maps[c, 1, z]
        for r, v in enumerate((mr * br + mi * bi, mr * bi - mi * br)):
            v = v.reshape(G, B, N)
            part[p, :, r] = v if c == 0 else part[p, :, r] + v

    near = [(a, b) for a in (-1, 0, 1) for b in (-1, 0, 1) if (a, b) != (0, 0)]

    def halo(dz, dx, p=0):
        if dz:
            a, b, n = (3, 0, 3) if dz < 0 else (8 + 2 * p, 11 + 2 * p, 2 - p)
            i = dx + 1 + 3 * (dz > 0) + 3 * p
        else:
            a, b, n = 3 + p, 3 + p, 1
            i = 9 + 2 * p + (dx + 1) // 2
        return pltpu.make_async_remote_copy(
            src_ref=big.at[1, :, pl.ds(a, n)], dst_ref=big.at[1 - dx, :, pl.ds(b, n)],
            send_sem=halo_send.at[i], recv_sem=halo_recv.at[i],
            device_id=near_id(dz, dx), device_id_type=MESH)

    def spread(p):
        def out(k):
            target = lax.rem(me_c + k + 1, G)
            pltpu.make_async_remote_copy(
                src_ref=part.at[p, target], dst_ref=sums.at[p, me_c], send_sem=rs_send, recv_sem=rs_recv.at[p],
                device_id={"coil": target}, device_id_type=MESH).start()

        loop(G - 1, out)
        sums[p, me_c] = part[p, me_c]

    def total(p):
        ref = sums.at[p, pl.ds(0, G - 1)]
        pltpu.make_async_copy(ref, ref, rs_recv.at[p]).wait()
        value = sums[p, 0]
        for k in range(1, G):
            value = value + sums[p, k]
        big[1, :, 3 + p] = value
        if p == 7:
            for dx in (0, -1, 1):
                halo(1, dx, 1).start()
        halo(0, -1, p).start()
        halo(0, 1, p).start()
        if p in (2, 6):
            for dx in (0, -1, 1):
                halo(-1 if p == 2 else 1, dx).start()
        combined[:, plane(p)] = value

    low_c, high_c, edge = me_c == 0, me_c == G - 1, (me_s == 0) | (me_s == G - 1)

    def guard(v, *outside):
        for out, here in outside:
            if here:
                v = jnp.where(out, 0.0, v)
        return v

    def layer0(z):
        rows = []
        for c in range(2):
            for blk in range(3):
                row = 2 - z if z < 3 else 24 - z if z >= 11 else z
                rows.append(guard(big[blk, c, row], (low_c, blk == 0), (high_c, blk == 2), (edge, z < 3)))
        f0h[:, z * N:(z + 1) * N], f0l[:, z * N:(z + 1) * N] = split(jnp.concatenate(rows, 0))

    def window(hi, lo, i, rows):
        h = [hi[rows, (2 * i + dz) * N:(2 * i + dz + 2) * N] for dz in range(3)]
        l = [lo[rows, (2 * i + dz) * N:(2 * i + dz + 2) * N] for dz in range(3)]
        return jnp.concatenate(h + l + h, 0)

    def conv1(i):
        data = window(f0h, f0l, i, slice(0, 48))
        for g in range(3):
            y = jnp.dot(w1[g * 384:(g + 1) * 384, 0:432], data, preferred_element_type=F32)
            for j in range(2):
                z = 2 * i + j
                v = jnp.maximum(shifted_sum(*[y[d * 128:(d + 1) * 128, j * N:(j + 1) * N] for d in range(3)]), 0.0)
                v = guard(v, (edge, z < 2))
                v = jnp.concatenate([
                    guard(v[:64], (low_c, g == 0)), guard(v[64:], (high_c, g == 2))], 0)
                at = (slice(g * 128, (g + 1) * 128), slice(z * N, (z + 1) * N))
                f1h[at], f1l[at] = split(v)

    def conv2(i):
        for g in range(5):
            data = window(f1h, f1l, i, slice(g * 64, g * 64 + 128))
            y = jnp.dot(w2[...], data, preferred_element_type=F32)
            for j in range(2):
                z = 2 * i + j
                v = jnp.maximum(shifted_sum(*[y[d * 64:(d + 1) * 64, j * N:(j + 1) * N] for d in range(3)]), 0.0)
                v = guard(v, (edge, z < 1))
                v = jnp.concatenate([
                    guard(v[:32], (low_c, g == 0)), guard(v[32:], (high_c, g == 4))], 0)
                at = (slice(g * 64, (g + 1) * 64), slice(z * N, (z + 1) * N))
                f2h[at], f2l[at] = split(v)

    def conv3(i):
        at = slice(2 * i * N, (2 * i + 2) * N)
        y = jnp.dot(w3[:, 0:320], f2h[:, at], preferred_element_type=F32)
        y = y[:144] + y[144:] + jnp.dot(w3[0:144, 0:320], f2l[:, at], preferred_element_type=F32)
        q3[2 * i] = y[:, :N]
        q3[2 * i + 1] = y[:, N:]

    def sides_in(*quarters):
        for p in quarters:
            halo(0, -1, p).wait_recv()
            halo(0, 1, p).wait_recv()

    def ends_in(dz, p=0):
        for dx in (-1, 0, 1):
            halo(dz, dx, p).wait_recv()

    def layers(planes, firsts, seconds):
        for z in planes:
            layer0(z)
        for i in firsts:
            conv1(i)
        for i in seconds:
            conv2(i)
        for i in seconds:
            conv3(i)

    def last(z):
        p = []
        for dy in range(3):
            p.append(sum(q3[z + dz, dz * 48 + dy * 16:dz * 48 + dy * 16 + 16, :] for dz in range(3)))
        v = shifted_sum(*p)
        for c in range(2):
            refined[c, plane(z)] = big[1, c, 3 + z] + v[c * B:(c + 1) * B]

    loop(B, lambda p: coil_back(0, p))
    for p in range(B):
        coil_back(1, p)
        spread(p)
        if p > 1:
            total(p - 2)
    sides_in(0, 1, 2, 3)
    ends_in(-1)
    layers(range(7), (0, 1), ())
    total(6)
    layers((), (), (0,))
    sides_in(4, 5)
    layers((7, 8), (2,), (1,))
    total(7)
    sides_in(6)
    layers((9,), (3,), (2,))
    for z in range(4):
        last(z)
    ends_in(1)
    layers((12, 13), (), ())
    sides_in(7)
    ends_in(1, 1)
    layers((10, 11), (4, 5), (3, 4))
    for z in range(4, B):
        last(z)

    for dz, dx in near:
        for p in range({-1: 1, 0: B, 1: 2}[dz]):
            halo(dz, dx, p).wait_send()

    def drain(ref, sem):
        pltpu.make_async_copy(ref, ref, sem).wait()

    drain(gath.at[:, pl.ds(0, G - 1)], ag_send)
    drain(send1.at[:, :, pl.ds(0, B * (CHUNK - ROWS))], a1_send)
    drain(send2.at[:, :, pl.ds(0, B * (CHUNK - ROWS))], a2_send)
    drain(part.at[:, pl.ds(0, G - 1)], rs_send)


def hand_over(a_in, b_in, a_out, b_out):
    a_out[...] = a_in[...]
    b_out[...] = b_in[...]


def body(estimate, coil_maps, measured, line_mask, w_first, w_middle, w_last):
    tabs = [jnp.asarray(t) for t in tables()]
    measured = measured.reshape(2, 2, N * B, N)
    w_first = jnp.transpose(w_first, (0, 2, 1))
    operands = (estimate, coil_maps, measured, line_mask, w_first, w_middle, w_last, *tabs)
    vmem = pl.BlockSpec(memory_space=pltpu.VMEM)
    dma = pltpu.SemaphoreType.DMA
    block = jax.ShapeDtypeStruct((2, B, B, N), F32)
    results = pl.pallas_call(
        kernel,
        out_shape=(block, block),
        in_specs=[pl.BlockSpec(memory_space=pl.ANY)] * len(operands),
        out_specs=(vmem, vmem),
        scratch_shapes=[pltpu.VMEM(a.shape, a.dtype) for a in (
            estimate, coil_maps, measured, line_mask, w_first, w_middle, w_last,
            tabs[0], tabs[1], tabs[2], tabs[3], tabs[4], tabs[5])] + [
            pltpu.VMEM((B, G, 2, B, N), F32),
            pltpu.VMEM((2, 2, N * B, N), F32),
            pltpu.VMEM((2, 2, N * B, N), F32),
            pltpu.VMEM((2, 2, N * B, N), F32),
            pltpu.VMEM((2, 2, N * B, N), F32),
            pltpu.VMEM((B, G, 2, B, N), F32),
            pltpu.VMEM((B, G, 2, B, N), F32),
            pltpu.VMEM((1152, 512), BF16),
            pltpu.VMEM((192, 1152), BF16),
            pltpu.VMEM((288, 384), BF16),
            pltpu.VMEM((3, 2, 14, B, N), F32),
            pltpu.VMEM((48, 14 * N), BF16), pltpu.VMEM((48, 14 * N), BF16),
            pltpu.VMEM((384, 12 * N), BF16), pltpu.VMEM((384, 12 * N), BF16),
            pltpu.VMEM((320, 10 * N), BF16), pltpu.VMEM((320, 10 * N), BF16),
            pltpu.VMEM((10, 144, N), F32),
            dma((13,)), dma, dma((B,)), dma, dma((2, B)), dma, dma((2, B)), dma, dma((B,)), dma((25,)), dma((25,)),
        ],
        compiler_params=pltpu.CompilerParams(
            collective_id=0, has_side_effects=True, vmem_limit_bytes=56 * 2**20),
    )(*operands)
    return pl.pallas_call(
        hand_over,
        out_shape=(block, block),
        in_specs=[vmem] * 2,
        out_specs=(vmem, vmem),
    )(*results)


def solution(mesh):
    in_specs = (
        P(None, "slab", "coil", None),
        P("coil", None, "slab", None, None),
        P("coil", None, None, "slab", None),
        P(),
        P(),
        P(),
        P(),
    )
    out_specs = (P(None, "slab", "coil", None), P(None, "slab", "coil", None))
    return jax.shard_map(body, mesh=mesh, in_specs=in_specs, out_specs=out_specs, check_vma=False)
```

time: 133 us -> 127 us (0.955)
  Pallas kernels: 133 us -> 126 us
    pallas_call x1, Pallas kernels: 5.09 us -> 1.53 us  [body(): pl.pallas_call(hand_over, out_shape=(block, block), in_specs=[vmem] * 2,...]
    pallas_call x1, Pallas kernels: 128 us -> 125 us  [body(): pl.pallas_call(kernel, out_shape=(block, block), in_specs=[pl.BlockSpec(m...]
where the time goes in v4:
time: 127 us
  Pallas kernels  126 us (99%)
    pallas_call x1, Pallas kernels, body(): pl.pallas_call(kernel, out_shape=(block, block), in_specs=[pl.BlockSpec(m...  125 us

profile of v4, /device:TPU:1, one launch (start us, length us, event | category | flops | bytes accessed | tf_op | source)
XLA Modules:
  0.0 126.9 jit_solution(9230758487456747915)
XLA Ops:
  0.6 124.8 %shard_map.140 = (f32[2,8,8,128]{3,2,1,0:T(8,128)}, f32[2,8,8,128]{3,2,1,0:T(8,128)}) custom-call(f32[2,8,8,128]{3,2,1,0:T(8,128)} %est_in.1, f32[2,2,8,128,128]{4,3,2,1,0:T(8,128)} %maps_in.1, f32[2,2,1024,128]{3,2,1,0:T(8,128)} %bitcast.2, s32[128,128]{1,0:T(8,128)} %mask_in.1, f32[27,2,32]{2,1,0:T(2,128)} %bitcast.3, f32[27,32,32]{2,1,0:T(8,128)} %wm_in.1, ...), custom_call_target="tpu_custom_call" | custom-call | tf_op jit(solution)/shard_map/pallas_call | solution.py:443
  125.4 1.5 %shard_map.141 = (f32[2,8,8,128]{3,2,1,0:T(8,128)}, f32[2,8,8,128]{3,2,1,0:T(8,128)}) custom-call(f32[2,8,8,128]{3,2,1,0:T(8,128)} %get-tuple-element.4.a_in, f32[2,8,8,128]{3,2,1,0:T(8,128)} %get-tuple-element.5.b_in), custom_call_target="tpu_custom_call" | custom-call | tf_op jit(solution)/shard_map/pallas_call | solution.py:471

commit v5 on v4

--- a/solution.py
+++ b/solution.py
@@ -74,13 +74,13 @@
     return p1 + down + up
 
 
-def build_weights(wf, wm, wl, w1, w2, w3, depth):
+def build_weights(wf, wm, wl, w1, w2, w3):
     lane = lax.broadcasted_iota(jnp.int32, (32, 512), 1)
     for dy in range(3):
         base = jnp.zeros((32, 512), F32)
         for dz in range(3):
             for dx in range(3):
-                taps = jnp.transpose(jnp.concatenate([wf[depth(dz) * 9 + dx * 3 + dy], jnp.zeros((6, 32), F32)], 0))
+                taps = jnp.transpose(jnp.concatenate([wf[dz * 9 + dx * 3 + dy], jnp.zeros((6, 32), F32)], 0))
                 for c in range(2):
                     base = jnp.where(lane == dz * 48 + c * 24 + dx + 5, taps[:, c:c + 1], base)
         hi = base.astype(BF16).astype(F32)
@@ -91,7 +91,7 @@
     for dz in range(3):
         for dy in range(3):
             base = jnp.concatenate(
-                [wm[depth(dz) * 9 + dx * 3 + dy] for dx in range(3)] + [jnp.zeros((32, 32), F32)], 1)
+                [wm[dz * 9 + dx * 3 + dy] for dx in range(3)] + [jnp.zeros((32, 32), F32)], 1)
             for xo in range(2):
                 hi, lo = split(pltpu.roll(base, 32, 1) if xo else base)
                 r = (dy * 2 + xo) * 32
@@ -100,7 +100,7 @@
     for dz in range(3):
         for dy in range(3):
             base = jnp.concatenate(
-                [wl[depth(dz) * 9 + dx * 3 + dy] for dx in range(3)] + [jnp.zeros((2, 416), F32)], 1)
+                [wl[dz * 9 + dx * 3 + dy] for dx in range(3)] + [jnp.zeros((2, 416), F32)], 1)
             both = jnp.concatenate([jnp.broadcast_to(base[o:o + 1], (8, 512)) for o in range(2)], 0)
             row = lax.broadcasted_iota(jnp.int32, (16, 512), 0) % 8
             moved = both
@@ -123,16 +123,17 @@
 ):
     me_c = lax.axis_index("coil")
     me_s = lax.axis_index("slab")
-    odd = lax.rem(me_s, 2)
-    sign = 1 - 2 * odd
-
-    def plane(t):
-        return (B - 1) * odd + sign * t
+
+    def plane(p):
+        return p // 2 + p % 2 * (B - 1 - p // 2 * 2)
 
     barrier = pltpu.get_barrier_semaphore()
 
     def near_id(dz, dx):
-        return {"coil": lax.rem(me_c + dx + G, G), "slab": lax.rem(me_s + sign * dz + G, G)}
+        return {"coil": lax.rem(me_c + dx + G, G), "slab": lax.rem(me_s + dz + G, G)}
+
+    def far_first(k):
+        return lax.rem(me_c + G // 2 + (k + 1) // 2 * (2 * lax.rem(k, 2) - 1) + G, G)
 
     def greet(target):
         pl.semaphore_signal(barrier, inc=1, device_id=target, device_id_type=MESH)
@@ -157,7 +158,7 @@
         def out(k):
             pltpu.make_async_remote_copy(
                 src_ref=est.at[:, q], dst_ref=gath.at[q, me_c], send_sem=ag_send, recv_sem=ag_recv.at[q],
-                device_id={"coil": lax.rem(me_c + k + 1, G)}, device_id_type=MESH).start()
+                device_id={"coil": far_first(k)}, device_id_type=MESH).start()
 
         loop(G - 1, out)
         gath[q, me_c] = est[:, q]
@@ -167,7 +168,7 @@
         pltpu.make_async_copy(ref, ref, ag_recv.at[q]).wait()
 
     def exchange(buf, dst, c, q, peer, send_sem, recv_sem, turned):
-        at = q + lax.rem(peer, 2) * (B - 1 - 2 * q) if turned else q
+        at = plane(q) if turned else q
         return pltpu.make_async_remote_copy(
             src_ref=buf.at[c, :, pl.ds(pl.multiple_of(at * CHUNK + peer * ROWS, ROWS), ROWS), :],
             dst_ref=dst.at[c, :, pl.ds(pl.multiple_of(at * CHUNK + me_s * ROWS, ROWS), ROWS), :],
@@ -202,20 +203,22 @@
         exchange_out(send1, recv1, c, q, a1_send, a1_recv)
 
     loads[0].wait()
-    gather_out(0)
-    gather_out(1)
+    for q in range(3):
+        gather_out(q)
     loads[1].wait()
     loads[2].wait()
     for q in range(B):
         gather_in(q)
-        if q + 2 < B:
-            gather_out(q + 2)
+        if q + 3 < B:
+            gather_out(q + 3)
         slab_plane(0, q)
-    loop(B, lambda q: slab_plane(1, q))
+        if q < 2:
+            slab_plane(1, q)
+    loop(B - 2, lambda q: slab_plane(1, q + 2))
 
     for load in loads[3:]:
         load.wait()
-    build_weights(wf, wm, wl, w1, w2, w3, lambda dz: 2 * odd + sign * dz)
+    build_weights(wf, wm, wl, w1, w2, w3)
 
     def pencils(c):
         loop(B, lambda q: exchange_in(recv1, c, q, a1_recv))
@@ -270,11 +273,11 @@
 
     def halo(dz, dx, p=0):
         if dz:
-            a, b, n = (3, 0, 3) if dz < 0 else (8 + 2 * p, 11 + 2 * p, 2 - p)
-            i = dx + 1 + 3 * (dz > 0) + 3 * p
+            a, b, n = (3, 11, 3) if dz < 0 else (8, 0, 3)
+            i = dx + 1 + 3 * (dz > 0)
         else:
-            a, b, n = 3 + p, 3 + p, 1
-            i = 9 + 2 * p + (dx + 1) // 2
+            a, b, n = 3 + plane(p), 3 + plane(p), 1
+            i = 6 + 2 * p + (dx + 1) // 2
         return pltpu.make_async_remote_copy(
             src_ref=big.at[1, :, pl.ds(a, n)], dst_ref=big.at[1 - dx, :, pl.ds(b, n)],
             send_sem=halo_send.at[i], recv_sem=halo_recv.at[i],
@@ -282,7 +285,7 @@
 
     def spread(p):
         def out(k):
-            target = lax.rem(me_c + k + 1, G)
+            target = far_first(k)
             pltpu.make_async_remote_copy(
                 src_ref=part.at[p, target], dst_ref=sums.at[p, me_c], send_sem=rs_send, recv_sem=rs_recv.at[p],
                 device_id={"coil": target}, device_id_type=MESH).start()
@@ -296,18 +299,15 @@
         value = sums[p, 0]
         for k in range(1, G):
             value = value + sums[p, k]
-        big[1, :, 3 + p] = value
-        if p == 7:
-            for dx in (0, -1, 1):
-                halo(1, dx, 1).start()
+        big[1, :, 3 + plane(p)] = value
         halo(0, -1, p).start()
         halo(0, 1, p).start()
-        if p in (2, 6):
+        if p in (4, 5):
             for dx in (0, -1, 1):
-                halo(-1 if p == 2 else 1, dx).start()
+                halo(2 * p - 9, dx).start()
         combined[:, plane(p)] = value
 
-    low_c, high_c, edge = me_c == 0, me_c == G - 1, (me_s == 0) | (me_s == G - 1)
+    low_c, high_c, low_s, high_s = me_c == 0, me_c == G - 1, me_s == 0, me_s == G - 1
 
     def guard(v, *outside):
         for out, here in outside:
@@ -315,12 +315,15 @@
                 v = jnp.where(out, 0.0, v)
         return v
 
-    def layer0(z):
+    def layer0(z, alone=False):
         rows = []
         for c in range(2):
             for blk in range(3):
-                row = 2 - z if z < 3 else 24 - z if z >= 11 else z
-                rows.append(guard(big[blk, c, row], (low_c, blk == 0), (high_c, blk == 2), (edge, z < 3)))
+                if alone and blk != 1:
+                    rows.append(jnp.zeros((B, N), F32))
+                    continue
+                rows.append(guard(
+                    big[blk, c, z], (low_c, blk == 0), (high_c, blk == 2), (low_s, z < 3), (high_s, z >= 11)))
         f0h[:, z * N:(z + 1) * N], f0l[:, z * N:(z + 1) * N] = split(jnp.concatenate(rows, 0))
 
     def window(hi, lo, i, rows):
@@ -328,27 +331,27 @@
         l = [lo[rows, (2 * i + dz) * N:(2 * i + dz + 2) * N] for dz in range(3)]
         return jnp.concatenate(h + l + h, 0)
 
-    def conv1(i):
+    def conv1(i, groups=(0, 1, 2)):
         data = window(f0h, f0l, i, slice(0, 48))
-        for g in range(3):
+        for g in groups:
             y = jnp.dot(w1[g * 384:(g + 1) * 384, 0:432], data, preferred_element_type=F32)
             for j in range(2):
                 z = 2 * i + j
                 v = jnp.maximum(shifted_sum(*[y[d * 128:(d + 1) * 128, j * N:(j + 1) * N] for d in range(3)]), 0.0)
-                v = guard(v, (edge, z < 2))
+                v = guard(v, (low_s, z < 2), (high_s, z >= 10))
                 v = jnp.concatenate([
                     guard(v[:64], (low_c, g == 0)), guard(v[64:], (high_c, g == 2))], 0)
                 at = (slice(g * 128, (g + 1) * 128), slice(z * N, (z + 1) * N))
                 f1h[at], f1l[at] = split(v)
 
-    def conv2(i):
-        for g in range(5):
+    def conv2(i, groups=(0, 1, 2, 3, 4)):
+        for g in groups:
             data = window(f1h, f1l, i, slice(g * 64, g * 64 + 128))
             y = jnp.dot(w2[...], data, preferred_element_type=F32)
             for j in range(2):
                 z = 2 * i + j
                 v = jnp.maximum(shifted_sum(*[y[d * 64:(d + 1) * 64, j * N:(j + 1) * N] for d in range(3)]), 0.0)
-                v = guard(v, (edge, z < 1))
+                v = guard(v, (low_s, z < 1), (high_s, z >= 9))
                 v = jnp.concatenate([
                     guard(v[:32], (low_c, g == 0)), guard(v[32:], (high_c, g == 4))], 0)
                 at = (slice(g * 64, (g + 1) * 64), slice(z * N, (z + 1) * N))
@@ -366,9 +369,9 @@
             halo(0, -1, p).wait_recv()
             halo(0, 1, p).wait_recv()
 
-    def ends_in(dz, p=0):
+    def ends_in(dz):
         for dx in (-1, 0, 1):
-            halo(dz, dx, p).wait_recv()
+            halo(dz, dx).wait_recv()
 
     def layers(planes, firsts, seconds):
         for z in planes:
@@ -386,7 +389,7 @@
             p.append(sum(q3[z + dz, dz * 48 + dy * 16:dz * 48 + dy * 16 + 16, :] for dz in range(3)))
         v = shifted_sum(*p)
         for c in range(2):
-            refined[c, plane(z)] = big[1, c, 3 + z] + v[c * B:(c + 1) * B]
+            refined[c, z] = big[1, c, 3 + z] + v[c * B:(c + 1) * B]
 
     loop(B, lambda p: coil_back(0, p))
     for p in range(B):
@@ -394,29 +397,22 @@
         spread(p)
         if p > 1:
             total(p - 2)
-    sides_in(0, 1, 2, 3)
+    sides_in(0, 1, 2, 3, 4)
     ends_in(-1)
-    layers(range(7), (0, 1), ())
+    layers((3, 4, 5, 9, 10, 11, 12, 13), (5,), ())
     total(6)
-    layers((), (), (0,))
-    sides_in(4, 5)
-    layers((7, 8), (2,), (1,))
+    sides_in(5)
+    layers((8,), (4,), (4,))
     total(7)
+    ends_in(1)
+    layers((0, 1, 2), (0, 1), (0,))
     sides_in(6)
-    layers((9,), (3,), (2,))
-    for z in range(4):
-        last(z)
-    ends_in(1)
-    layers((12, 13), (), ())
-    sides_in(7)
-    ends_in(1, 1)
-    layers((10, 11), (4, 5), (3, 4))
-    for z in range(4, B):
-        last(z)
-
-    for dz, dx in near:
-        for p in range({-1: 1, 0: B, 1: 2}[dz]):
-            halo(dz, dx, p).wait_send()
+    layer0(6)
+    layer0(7, True)
+    conv1(2, (1,))
+    conv1(3, (1,))
+    for i in (1, 2, 3):
+        conv2(i, (2,))
 
     def drain(ref, sem):
         pltpu.make_async_copy(ref, ref, sem).wait()
@@ -425,6 +421,19 @@
     drain(send1.at[:, :, pl.ds(0, B * (CHUNK - ROWS))], a1_send)
     drain(send2.at[:, :, pl.ds(0, B * (CHUNK - ROWS))], a2_send)
     drain(part.at[:, pl.ds(0, G - 1)], rs_send)
+    for dz, dx in near:
+        for p in range(1 if dz else B):
+            halo(dz, dx, p).wait_send()
+    sides_in(7)
+    layer0(7)
+    conv1(2, (0, 2))
+    conv1(3, (0, 2))
+    for i in (1, 2, 3):
+        conv2(i, (0, 1, 3, 4))
+    for i in (1, 2, 3):
+        conv3(i)
+    for z in range(B):
+        last(z)
 
 
 def hand_over(a_in, b_in, a_out, b_out):
@@ -463,7 +472,7 @@
             pltpu.VMEM((384, 12 * N), BF16), pltpu.VMEM((384, 12 * N), BF16),
             pltpu.VMEM((320, 10 * N), BF16), pltpu.VMEM((320, 10 * N), BF16),
             pltpu.VMEM((10, 144, N), F32),
-            dma((13,)), dma, dma((B,)), dma, dma((2, B)), dma, dma((2, B)), dma, dma((B,)), dma((25,)), dma((25,)),
+            dma((13,)), dma, dma((B,)), dma, dma((2, B)), dma, dma((2, B)), dma, dma((B,)), dma((22,)), dma((22,)),
         ],
         compiler_params=pltpu.CompilerParams(
             collective_id=0, has_side_effects=True, vmem_limit_bytes=56 * 2**20),

time: 127 us -> 127 us (level)
  no operation moved by 1% of the time
where the time goes in v5:
time: 127 us
  Pallas kernels  126 us (99%)
    pallas_call x1, Pallas kernels, body(): pl.pallas_call(kernel, out_shape=(block, block), in_specs=[pl.BlockSpec(m...  125 us

profile of v5, /device:TPU:1, one launch (start us, length us, event | category | flops | bytes accessed | tf_op | source)
XLA Modules:
  0.0 126.7 jit_solution(2749898781502116556)
XLA Ops:
  0.6 124.5 %shard_map.140 = (f32[2,8,8,128]{3,2,1,0:T(8,128)}, f32[2,8,8,128]{3,2,1,0:T(8,128)}) custom-call(f32[2,8,8,128]{3,2,1,0:T(8,128)} %est_in.1, f32[2,2,8,128,128]{4,3,2,1,0:T(8,128)} %maps_in.1, f32[2,2,1024,128]{3,2,1,0:T(8,128)} %bitcast.2, s32[128,128]{1,0:T(8,128)} %mask_in.1, f32[27,2,32]{2,1,0:T(2,128)} %bitcast.3, f32[27,32,32]{2,1,0:T(8,128)} %wm_in.1, ...), custom_call_target="tpu_custom_call" | custom-call | tf_op jit(solution)/shard_map/pallas_call | solution.py:452
  125.2 1.5 %shard_map.141 = (f32[2,8,8,128]{3,2,1,0:T(8,128)}, f32[2,8,8,128]{3,2,1,0:T(8,128)}) custom-call(f32[2,8,8,128]{3,2,1,0:T(8,128)} %get-tuple-element.4.a_in, f32[2,8,8,128]{3,2,1,0:T(8,128)} %get-tuple-element.5.b_in), custom_call_target="tpu_custom_call" | custom-call | tf_op jit(solution)/shard_map/pallas_call | solution.py:480

commit v6 on v5

--- a/solution.py
+++ b/solution.py
@@ -436,11 +436,6 @@
         last(z)
 
 
-def hand_over(a_in, b_in, a_out, b_out):
-    a_out[...] = a_in[...]
-    b_out[...] = b_in[...]
-
-
 def body(estimate, coil_maps, measured, line_mask, w_first, w_middle, w_last):
     tabs = [jnp.asarray(t) for t in tables()]
     measured = measured.reshape(2, 2, N * B, N)
@@ -448,8 +443,8 @@
     operands = (estimate, coil_maps, measured, line_mask, w_first, w_middle, w_last, *tabs)
     vmem = pl.BlockSpec(memory_space=pltpu.VMEM)
     dma = pltpu.SemaphoreType.DMA
-    block = jax.ShapeDtypeStruct((2, B, B, N), F32)
-    results = pl.pallas_call(
+    block = pltpu.VMEM((2, B, B, N), F32)
+    return pl.pallas_call(
         kernel,
         out_shape=(block, block),
         in_specs=[pl.BlockSpec(memory_space=pl.ANY)] * len(operands),
@@ -477,12 +472,6 @@
         compiler_params=pltpu.CompilerParams(
             collective_id=0, has_side_effects=True, vmem_limit_bytes=56 * 2**20),
     )(*operands)
-    return pl.pallas_call(
-        hand_over,
-        out_shape=(block, block),
-        in_specs=[vmem] * 2,
-        out_specs=(vmem, vmem),
-    )(*results)
 
 
 def solution(mesh):

time: 127 us -> 126 us (level)
  Pallas kernels: 126 us -> 124 us
    pallas_call x1 -> x0, Pallas kernels: 1.53 us -> none  [body(): pl.pallas_call(hand_over, out_shape=(block, block), in_specs=[vmem] * 2,...]
where the time goes in v6:
time: 126 us
  Pallas kernels  124 us (98%)
  local copies, waits for them, and re-layouts  1.26 us (1%)
    pallas_call x1, Pallas kernels, body(): pl.pallas_call(kernel, out_shape=(block, block), in_specs=[pl.BlockSpec(m...  124 us

profile of v6, /device:TPU:1, one launch (start us, length us, event | category | flops | bytes accessed | tf_op | source)
XLA Modules:
  0.0 125.8 jit_solution(8260040934223495949)
XLA Ops:
  0.6 123.9 %shard_map.140 = (f32[2,8,8,128]{3,2,1,0:T(8,128)S(1)}, f32[2,8,8,128]{3,2,1,0:T(8,128)S(1)}) custom-call(f32[2,8,8,128]{3,2,1,0:T(8,128)} %est_in.1, f32[2,2,8,128,128]{4,3,2,1,0:T(8,128)} %maps_in.1, f32[2,2,1024,128]{3,2,1,0:T(8,128)} %bitcast.2, s32[128,128]{1,0:T(8,128)} %mask_in.1, f32[27,2,32]{2,1,0:T(2,128)} %bitcast.3, f32[27,32,32]{2,1,0:T(8,128)} %wm_in.1, ...), custom_call_target="tpu_custom_call" | custom-call | tf_op jit(solution)/shard_map/pallas_call | solution.py:447
  124.5 0.6 copy.17
  125.2 0.6 copy.18

commit v7 on v6

--- a/solution.py
+++ b/solution.py
@@ -118,7 +118,7 @@
     est, maps, meas, mask, wf, wm, wl, lf, li, rf, ri_, lzf, lzi,
     gath, send1, recv1, send2, recv2, part, sums,
     w1, w2, w3, big, f0h, f0l, f1h, f1l, f2h, f2l, q3,
-    load_sem, ag_send, ag_recv, a1_send, a1_recv, a2_send, a2_recv,
+    go, load_sem, ag_send, ag_recv, a1_send, a1_recv, a2_send, a2_recv,
     rs_send, rs_recv, halo_send, halo_recv,
 ):
     me_c = lax.axis_index("coil")
@@ -135,24 +135,44 @@
     def far_first(k):
         return lax.rem(me_c + G // 2 + (k + 1) // 2 * (2 * lax.rem(k, 2) - 1) + G, G)
 
-    def greet(target):
-        pl.semaphore_signal(barrier, inc=1, device_id=target, device_id_type=MESH)
-
-    def greet_lines(k):
-        greet({"coil": lax.rem(me_c + k + 1, G)})
-        greet({"slab": lax.rem(me_s + k + 1, G)})
-
-    loop(G - 1, greet_lines)
-    for dz in (-1, 1):
-        for dx in (-1, 1):
-            greet(near_id(dz, dx))
+    def greet(sem, target):
+        pl.semaphore_signal(sem, inc=1, device_id=target, device_id_type=MESH)
+
+    core = lax.rem(me_c, 2)
+    chip = me_c // 2
+    sibling = {"coil": me_c + 1 - 2 * core}
+    loop(G - 1, lambda k: greet(barrier, {"coil": 2 * chip + 1, "slab": lax.rem(me_s + k + 1, G)}))
+    loop(7, lambda k: greet(barrier, {"coil": 2 * lax.rem(chip + k + 1, 8)}))
+
+    @pl.when(core == 1)
+    def _():
+        greet(barrier, sibling)
 
     pairs = [(est_in, est), (t0, lf), (maps_in, maps), (wf_in, wf), (wm_in, wm), (wl_in, wl), (t2, rf), (t4, lzf),
              (meas_in, meas), (mask_in, mask), (t5, lzi), (t3, ri_), (t1, li)]
     loads = [pltpu.make_async_copy(a, b, load_sem.at[i]) for i, (a, b) in enumerate(pairs)]
     for load in loads:
         load.start()
-    pl.semaphore_wait(barrier, 2 * (G - 1) + 4)
+
+    @pl.when(core == 0)
+    def _():
+        pl.semaphore_wait(barrier, G - 1)
+        greet(go, sibling)
+
+    @pl.when(core == 1)
+    def _():
+        pl.semaphore_wait(go, 1)
+
+    def slabs_ready():
+        @pl.when(core == 1)
+        def _():
+            pl.semaphore_wait(barrier, 2 * (G - 1))
+            greet(go, sibling)
+
+        @pl.when(core == 0)
+        def _():
+            pl.semaphore_wait(go, 1)
+
 
     def gather_out(q):
         def out(k):
@@ -192,7 +212,7 @@
         ref = all_of(dst, c, q)
         pltpu.make_async_copy(ref, ref, recv_sem.at[c, q]).wait()
 
-    def slab_plane(c, q):
+    def slab_plane(c, q, first=False):
         ir = gath[q, :, 0].reshape(N, N)
         ii = gath[q, :, 1].reshape(N, N)
         mr = maps[c, 0, q]
@@ -200,6 +220,8 @@
         y = left(lf[...], jnp.concatenate([mr * ir - mi * ii, mr * ii + mi * ir], 0))
         for r in range(2):
             send1[c, r, pl.ds(pl.multiple_of(q * CHUNK, CHUNK), CHUNK), :] = y[r * N:(r + 1) * N]
+        if first:
+            slabs_ready()
         exchange_out(send1, recv1, c, q, a1_send, a1_recv)
 
     loads[0].wait()
@@ -211,7 +233,7 @@
         gather_in(q)
         if q + 3 < B:
             gather_out(q + 3)
-        slab_plane(0, q)
+        slab_plane(0, q, q == 0)
         if q < 2:
             slab_plane(1, q)
     loop(B - 2, lambda q: slab_plane(1, q + 2))
@@ -467,7 +489,7 @@
             pltpu.VMEM((384, 12 * N), BF16), pltpu.VMEM((384, 12 * N), BF16),
             pltpu.VMEM((320, 10 * N), BF16), pltpu.VMEM((320, 10 * N), BF16),
             pltpu.VMEM((10, 144, N), F32),
-            dma((13,)), dma, dma((B,)), dma, dma((2, B)), dma, dma((2, B)), dma, dma((B,)), dma((22,)), dma((22,)),
+            pltpu.SemaphoreType.REGULAR, dma((13,)), dma, dma((B,)), dma, dma((2, B)), dma, dma((2, B)), dma, dma((B,)), dma((22,)), dma((22,)),
         ],
         compiler_params=pltpu.CompilerParams(
             collective_id=0, has_side_effects=True, vmem_limit_bytes=56 * 2**20),

time: 126 us -> 124 us (0.984)
  Pallas kernels: 124 us -> 122 us
    pallas_call x1, Pallas kernels: 124 us -> 122 us  [body(): pl.pallas_call(kernel, out_shape=(block, block), in_specs=[pl.BlockSpec(m...]
where the time goes in v7:
time: 124 us
  Pallas kernels  122 us (98%)
  local copies, waits for them, and re-layouts  1.26 us (1%)
    pallas_call x1, Pallas kernels, body(): pl.pallas_call(kernel, out_shape=(block, block), in_specs=[pl.BlockSpec(m...  122 us

profile of v7, /device:TPU:1, one launch (start us, length us, event | category | flops | bytes accessed | tf_op | source)
XLA Modules:
  0.0 123.8 jit_solution(4484729034562236311)
XLA Ops:
  0.6 121.9 %shard_map.140 = (f32[2,8,8,128]{3,2,1,0:T(8,128)S(1)}, f32[2,8,8,128]{3,2,1,0:T(8,128)S(1)}) custom-call(f32[2,8,8,128]{3,2,1,0:T(8,128)} %est_in.1, f32[2,2,8,128,128]{4,3,2,1,0:T(8,128)} %maps_in.1, f32[2,2,1024,128]{3,2,1,0:T(8,128)} %bitcast.2, s32[128,128]{1,0:T(8,128)} %mask_in.1, f32[27,2,32]{2,1,0:T(2,128)} %bitcast.3, f32[27,32,32]{2,1,0:T(8,128)} %wm_in.1, ...), custom_call_target="tpu_custom_call" | custom-call | tf_op jit(solution)/shard_map/pallas_call | solution.py:469
  122.6 0.6 copy.17
  123.2 0.6 copy.18
